TPU v7x, 128 devices: a whole 4x4x4 slice. The times are simulated.
128 devices in a mesh: px: 8 (over x, core), py: 16 (over z, y).
Axes of the slice: x: 4, y: 4, z: 4, core: 2. Of those that a mesh axis runs over, the one named last changes fastest.
Arguments:
- incident_power_density: float32 [3, 2048, 2048], P(None, ('px', 'py')), may hold values from 0.1 to 4
- coupling_patch_locator: int32 [8, 256, 2048], P(None, 'px', 'py'), may hold values from 0 to 32767, as said below
- coupling_share_factor: float32 [8, 256, 2048], P(None, 'px', 'py'), may hold values from 0.05 to 1
- starting_warmth: float32 [24, 256, 2048], P(None, 'px', 'py'), may hold values from -6 to 6
- diffusive_coefficient: float32 [24, 256, 2048], P(None, 'px', 'py'), may hold values from 0.3 to 3
- thermal_storage: float32 [24, 256, 2048], P(None, 'px', 'py'), may hold values from 0.05 to 0.5
Outputs:
- final_warmth: float32 [24, 256, 2048], P(None, 'px', 'py')
- leftover_error_vector: float32 [24, 256, 2048], P(None, 'px', 'py')
Inputs may be any that keep to these rules, and one draw needn't show every extreme that they name: `coupling_patch_locator`: every index lies in the window of the cell's own part, near the tile that faces the cell.
All inputs are finite; a program needn't handle non-finite values.
Results may differ from a plain program's by a relative error of at most 0.00019.
Values sent between devices are 32-bit elements; how exact they have to be, the bound alone decides.
A program may use at most 128 MiB of HBM per device.

v0:
```python
import jax
import jax.numpy as jnp
from jax import lax
from jax.sharding import PartitionSpec as P

ITERS = 2


through_ratio = 0.5


def extended(block, sides, width):
    for axis, dim in sides:
        count = lax.axis_size(axis)
        forward = [(i, i + 1) for i in range(count - 1)]
        backward = [(target, source) for source, target in forward]
        low = lax.ppermute(
            lax.slice_in_dim(block, block.shape[dim] - width, None, axis=dim), axis, forward
        )
        high = lax.ppermute(lax.slice_in_dim(block, 0, width, axis=dim), axis, backward)
        block = jnp.concatenate([low, block, high], axis=dim)
    return block


def with_rim(field):
    rimmed = extended(field, (("px", 1), ("py", 2)), 1)
    return jnp.pad(rimmed, ((1, 1), (0, 0), (0, 0)))


def stencil(padded, field, faces, diagonal):
    beside = faces[0] * padded[:-2, 1:-1, 1:-1] + faces[1] * padded[2:, 1:-1, 1:-1]
    beside = beside + faces[2] * padded[1:-1, :-2, 1:-1] + faces[3] * padded[1:-1, 2:, 1:-1]
    beside = beside + faces[4] * padded[1:-1, 1:-1, :-2] + faces[5] * padded[1:-1, 1:-1, 2:]
    return diagonal * field - beside


def operate(field, faces, diagonal):
    return stencil(with_rim(field), field, faces, diagonal)


def face_terms(centre, padded):
    return (
        through_ratio * 0.5 * (centre + padded[:-2, 1:-1, 1:-1]),
        through_ratio * 0.5 * (centre + padded[2:, 1:-1, 1:-1]),
        0.5 * (centre + padded[1:-1, :-2, 1:-1]),
        0.5 * (centre + padded[1:-1, 2:, 1:-1]),
        0.5 * (centre + padded[1:-1, 1:-1, :-2]),
        0.5 * (centre + padded[1:-1, 1:-1, 2:]),
    )


def surface_flux(window, coupling_patch_locator, coupling_share_factor):
    flat = window.reshape(-1)
    values = flat[coupling_patch_locator]
    return jnp.sum(coupling_share_factor * values, axis=0)


def preconditioned_product(leftover_error_vector, scaled):
    return lax.psum(jnp.sum(leftover_error_vector * scaled), ("px", "py"))


def curvature_product(axis_direction, image):
    return lax.psum(jnp.sum(axis_direction * image), ("px", "py"))


def solve_step(solution, leftover_error_vector, faces, diagonal, apply, mask):
    scaled = mask * (leftover_error_vector / diagonal)
    axis_direction = scaled
    gamma = preconditioned_product(leftover_error_vector, scaled)
    for turn in range(ITERS):
        image = apply(axis_direction, faces, diagonal)
        alpha = gamma / curvature_product(axis_direction, image)
        solution = solution + alpha * axis_direction
        leftover_error_vector = leftover_error_vector - alpha * image
        if turn + 1 < ITERS:
            scaled = mask * (leftover_error_vector / diagonal)
            fresh = preconditioned_product(leftover_error_vector, scaled)
            axis_direction = scaled + fresh / gamma * axis_direction
            gamma = fresh
    return (solution, leftover_error_vector)


def body(
    incident_power_density,
    coupling_patch_locator,
    coupling_share_factor,
    starting_warmth,
    diffusive_coefficient,
    thermal_storage,
):
    sheet_level = starting_warmth.shape[0]
    rimmed = extended(diffusive_coefficient, (("px", 1), ("py", 2)), 1)
    padded = jnp.pad(rimmed, ((1, 1), (0, 0), (0, 0)))
    faces = face_terms(diffusive_coefficient, padded)
    diagonal = thermal_storage + faces[0] + faces[1] + faces[2] + faces[3] + faces[4] + faces[5]
    mask = jnp.ones((1, 1, 1), jnp.float32)
    frames = incident_power_density.shape[0]
    final_warmth = starting_warmth
    leftover_error_vector = starting_warmth
    for frame in range(frames):
        window = lax.all_to_all(
            incident_power_density[frame : frame + 1], "py", split_axis=2, concat_axis=1, tiled=True
        )[0]
        flux = surface_flux(window, coupling_patch_locator, coupling_share_factor)
        solution = final_warmth
        right = thermal_storage * final_warmth
        right = right.at[sheet_level - 1].add(flux)
        leftover_error_vector = right - operate(solution, faces, diagonal)
        final_warmth, leftover_error_vector = solve_step(
            solution, leftover_error_vector, faces, diagonal, operate, mask
        )
    return (final_warmth, leftover_error_vector)


def solution(mesh):
    placed = (
        P(None, ("px", "py"), None),
        P(None, "px", "py"),
        P(None, "px", "py"),
        P(None, "px", "py"),
        P(None, "px", "py"),
        P(None, "px", "py"),
    )
    return jax.shard_map(
        body,
        mesh=mesh,
        in_specs=placed,
        out_specs=(P(None, "px", "py"), P(None, "px", "py")),
        check_vma=False,
    )
```

profile of v0, /device:TPU:0, one launch (start us, length us, event | category | flops | bytes accessed | tf_op | source)
XLA Modules:
  0.0 1495.4 jit_solution(4110255874786260292)
XLA Ops:
  5.2 4.8 collective-permute-start
  13.5 9.3 reduce.10
  23.9 8.5 all-to-all-start.1
  33.9 9.3 reduce.8
  44.8 9.3 reduce.6
  68.7 9.7 all-to-all-start
  80.0 9.8 all-to-all-done
  89.8 6.9 all-to-all-start.2
  105.1 180.5 %gather_fusion.1 = f32[32768]{0:T(1024)S(1)} fusion(f32[32768]{0:T(1024)S(1)} %bitcast.28, s32[32768]{0:T(1024)S(1)} %broadcast_clamp_fusion), kind=kCustom, calls=%fused_computation.1 | custom fusion | bytes 393216 | tf_op jit(solution)/shard_map/gather | solution.py:54
  285.7 180.5 %gather_fusion = f32[32768]{0:T(1024)S(1)} fusion(f32[32768]{0:T(1024)S(1)} %bitcast.29, s32[32768]{0:T(1024)S(1)} %broadcast_clamp_fusion), kind=kCustom, calls=%fused_computation | custom fusion | bytes 393216 | tf_op jit(solution)/shard_map/gather | solution.py:54
  469.6 180.5 %gather_fusion.2 = f32[32768]{0:T(1024)S(1)} fusion(f32[32768]{0:T(1024)S(1)} %bitcast.30, s32[32768]{0:T(1024)S(1)} %broadcast_clamp_fusion), kind=kCustom, calls=%fused_computation.2 | custom fusion | bytes 393216 | tf_op jit(solution)/shard_map/gather | solution.py:54
  669.1 8.7 collective-permute-done.10
  677.9 4.8 collective-permute-done.11
  685.3 68.3 %all-reduce.12 = (f32[]{:T(128)}, f32[]{:T(128)}) all-reduce(f32[]{:T(128)} %get-tuple-element.43, f32[]{:T(128)} %get-tuple-element.42), channel_id=1, replica_groups=mesh['px'=8,'py'=16] {'px','py'}, use_global_device_ids=true, to_apply=%region_2.3 | all-reduce | flops 2 | bytes 16 | tf_op jit(solution)/shard_map/psum | solution.py:59
  756.7 64.2 %psum.86 = f32[]{:T(128)} all-reduce(f32[]{:T(128)} %multiply_reduce_fusion.7), channel_id=1, replica_groups=mesh['px'=8,'py'=16] {'px','py'}, use_global_device_ids=true, to_apply=%region_6.7 | all-reduce | flops 1 | bytes 8 | tf_op jit(solution)/shard_map/psum | solution.py:59
  832.0 8.7 collective-permute-done.14
  840.7 4.8 collective-permute-done.15
  847.4 68.5 %psum.87 = f32[]{:T(128)} all-reduce(f32[]{:T(128)} %fusion.69), channel_id=1, replica_groups=mesh['px'=8,'py'=16] {'px','py'}, use_global_device_ids=true, to_apply=%region_8.9 | all-reduce | flops 1 | bytes 8 | tf_op jit(solution)/shard_map/psum | solution.py:63
  928.4 8.7 collective-permute-done.18
  956.2 8.7 collective-permute-done.22
  972.4 68.9 %all-reduce.11 = (f32[]{:T(128)}, f32[]{:T(128)}) all-reduce(f32[]{:T(128)} %get-tuple-element.41, f32[]{:T(128)} %get-tuple-element.40), channel_id=1, replica_groups=mesh['px'=8,'py'=16] {'px','py'}, use_global_device_ids=true, to_apply=%region_11.12 | all-reduce | flops 2 | bytes 16 | tf_op jit(solution)/shard_map/psum | solution.py:59
  1044.2 63.8 %psum.90 = f32[]{:T(128)} all-reduce(f32[]{:T(128)} %multiply_reduce_fusion.4), channel_id=1, replica_groups=mesh['px'=8,'py'=16] {'px','py'}, use_global_device_ids=true, to_apply=%region_15.16 | all-reduce | flops 1 | bytes 8 | tf_op jit(solution)/shard_map/psum | solution.py:59
  1119.5 8.5 collective-permute-done.26
  1128.0 4.8 collective-permute-done.27
  1134.7 68.3 %psum.91 = f32[]{:T(128)} all-reduce(f32[]{:T(128)} %fusion.36), channel_id=1, replica_groups=mesh['px'=8,'py'=16] {'px','py'}, use_global_device_ids=true, to_apply=%region_17.18 | all-reduce | flops 1 | bytes 8 | tf_op jit(solution)/shard_map/psum | solution.py:63
  1215.5 8.7 collective-permute-done.30
  1243.2 8.7 collective-permute-done.34
  1259.4 68.9 %all-reduce.10 = (f32[]{:T(128)}, f32[]{:T(128)}) all-reduce(f32[]{:T(128)} %get-tuple-element.39, f32[]{:T(128)} %get-tuple-element.38), channel_id=1, replica_groups=mesh['px'=8,'py'=16] {'px','py'}, use_global_device_ids=true, to_apply=%region_20.21 | all-reduce | flops 2 | bytes 16 | tf_op jit(solution)/shard_map/psum | solution.py:59
  1332.2 63.8 %psum.94 = f32[]{:T(128)} all-reduce(f32[]{:T(128)} %get-tuple-element.55), channel_id=1, replica_groups=mesh['px'=8,'py'=16] {'px','py'}, use_global_device_ids=true, to_apply=%region_24.25 | all-reduce | flops 1 | bytes 8 | tf_op jit(solution)/shard_map/psum | solution.py:59
  1407.0 8.7 collective-permute-done.38
  1415.8 4.8 collective-permute-done.39
  1423.2 68.5 %psum.95 = f32[]{:T(128)} all-reduce(f32[]{:T(128)} %get-tuple-element.53), channel_id=1, replica_groups=mesh['px'=8,'py'=16] {'px','py'}, use_global_device_ids=true, to_apply=%region_26.27 | all-reduce | flops 1 | bytes 8 | tf_op jit(solution)/shard_map/psum | solution.py:63
  (198 shorter events, 180.9 us)
Async XLA Ops:
  1.6 53.6 %collective-permute-start.4 = (f32[24,1,128]{2,1,0:T(1,128)S(1)}, f32[24,1,128]{2,1,0:T(1,128)S(1)}, u32[]{:S(2)}, u32[]{:S(2)}) collective-permute-start(f32[24,1,128]{2,1,0:T(1,128)S(1)} %get-tuple-element.114), channel_id=1, source_target_pairs={{0,16},{16,32},{32,48},{48,64},{64,80},{80,96},{96,112},{1,17},{17... | collective-permute-start | bytes 36872 | tf_op jit(solution)/shard_map/ppermute | solution.py:17
  2.9 52.3 %collective-permute-start.5 = (f32[24,1,128]{2,1,0:T(1,128)S(1)}, f32[24,1,128]{2,1,0:T(1,128)S(1)}, u32[]{:S(2)}, u32[]{:S(2)}) collective-permute-start(f32[24,1,128]{2,1,0:T(1,128)S(1)} %get-tuple-element.115), channel_id=1, source_target_pairs={{16,0},{32,16},{48,32},{64,48},{80,64},{96,80},{112,96},{17,1},{33... | collective-permute-start | bytes 36872 | tf_op jit(solution)/shard_map/ppermute | solution.py:20
  5.2 56.4 %collective-permute-start = (f32[24,1,128]{2,1,0:T(1,128)S(1)}, f32[24,1,128]{2,1,0:T(1,128)S(1)}, u32[]{:S(2)}, u32[]{:S(2)}) collective-permute-start(f32[24,1,128]{2,1,0:T(1,128)S(1)} %get-tuple-element.112), channel_id=1, source_target_pairs={{0,16},{16,32},{32,48},{48,64},{64,80},{80,96},{96,112},{1,17},{17... | collective-permute-start | bytes 36872 | tf_op jit(solution)/shard_map/ppermute | solution.py:17
  10.0 51.6 %collective-permute-start.1 = (f32[24,1,128]{2,1,0:T(1,128)S(1)}, f32[24,1,128]{2,1,0:T(1,128)S(1)}, u32[]{:S(2)}, u32[]{:S(2)}) collective-permute-start(f32[24,1,128]{2,1,0:T(1,128)S(1)} %get-tuple-element.113), channel_id=1, source_target_pairs={{16,0},{32,16},{48,32},{64,48},{80,64},{96,80},{112,96},{17,1},{33... | collective-permute-start | bytes 36872 | tf_op jit(solution)/shard_map/ppermute | solution.py:20
  23.9 44.8 %all-to-all-start.1 = ((f32[16,1,2048]{2,1,0:T(1,128)}), f32[16,1,2048]{2,1,0:T(1,128)S(1)}, u32[]{:S(2)}, u32[]{:S(2)}) async-start(f32[16,1,2048]{2,1,0:T(1,128)} %reshape.134), calls=%async_computation.1 | async-start | bytes 262144 | tf_op jit(solution)/shard_map/all_to_all | solution.py:101
  56.3 22.1 %collective-permute-start.6 = (f32[24,34,1]{2,1,0:T(8,128)}, f32[24,34,1]{2,1,0:T(8,128)S(1)}, u32[]{:S(2)}, u32[]{:S(2)}) collective-permute-start(f32[24,34,1]{2,1,0:T(8,128)} %get-tuple-element.94), channel_id=1, source_target_pairs={{0,1},{1,2},{2,3},{3,4},{4,5},{5,6},{6,7},{7,8},{8,9},{9,10},{10,1... | collective-permute-start | bytes 9800 | tf_op jit(solution)/shard_map/ppermute | solution.py:17
  60.3 18.1 %collective-permute-start.7 = (f32[24,34,1]{2,1,0:T(8,128)}, f32[24,34,1]{2,1,0:T(8,128)S(1)}, u32[]{:S(2)}, u32[]{:S(2)}) collective-permute-start(f32[24,34,1]{2,1,0:T(8,128)} %get-tuple-element.95), channel_id=1, source_target_pairs={{1,0},{2,1},{3,2},{4,3},{5,4},{6,5},{7,6},{8,7},{9,8},{10,9},{11,1... | collective-permute-start | bytes 9800 | tf_op jit(solution)/shard_map/ppermute | solution.py:20
  62.8 33.9 %collective-permute-start.2 = (f32[24,34,1]{2,1,0:T(8,128)}, f32[24,34,1]{2,1,0:T(8,128)S(1)}, u32[]{:S(2)}, u32[]{:S(2)}) collective-permute-start(f32[24,34,1]{2,1,0:T(8,128)} %get-tuple-element.92), channel_id=1, source_target_pairs={{0,1},{1,2},{2,3},{3,4},{4,5},{5,6},{6,7},{7,8},{8,9},{9,10},{10,1... | collective-permute-start | bytes 9800 | tf_op jit(solution)/shard_map/ppermute | solution.py:17
  67.4 29.3 %collective-permute-start.3 = (f32[24,34,1]{2,1,0:T(8,128)}, f32[24,34,1]{2,1,0:T(8,128)S(1)}, u32[]{:S(2)}, u32[]{:S(2)}) collective-permute-start(f32[24,34,1]{2,1,0:T(8,128)} %get-tuple-element.93), channel_id=1, source_target_pairs={{1,0},{2,1},{3,2},{4,3},{5,4},{6,5},{7,6},{8,7},{9,8},{10,9},{11,1... | collective-permute-start | bytes 9800 | tf_op jit(solution)/shard_map/ppermute | solution.py:20
  68.7 21.1 %all-to-all-start = ((f32[16,1,2048]{2,1,0:T(1,128)}), f32[16,1,2048]{2,1,0:T(1,128)S(1)}, u32[]{:S(2)}, u32[]{:S(2)}) async-start(f32[16,1,2048]{2,1,0:T(1,128)} %reshape.132), calls=%async_computation | async-start | bytes 262144 | tf_op jit(solution)/shard_map/all_to_all | solution.py:101
  89.8 376.4 %all-to-all-start.2 = ((f32[16,1,2048]{2,1,0:T(1,128)}), f32[16,1,2048]{2,1,0:T(1,128)S(1)}, u32[]{:S(2)}, u32[]{:S(2)}) async-start(f32[16,1,2048]{2,1,0:T(1,128)} %reshape.130), calls=%async_computation.2 | async-start | bytes 262144 | tf_op jit(solution)/shard_map/all_to_all | solution.py:101
  658.6 5.0 collective-permute-start.9
  663.9 14.0 collective-permute-start.10
  667.8 14.8 collective-permute-start.11
  829.1 11.7 collective-permute-start.14
  830.7 14.8 collective-permute-start.15
  920.5 4.5 collective-permute-start.17
  925.3 11.8 collective-permute-start.18
  927.1 14.8 collective-permute-start.19
  946.3 4.9 collective-permute-start.21
  951.5 13.4 collective-permute-start.22
  954.9 14.8 collective-permute-start.23
  1116.2 11.8 collective-permute-start.26
  1118.0 14.8 collective-permute-start.27
  1207.5 4.5 collective-permute-start.29
  1212.4 11.8 collective-permute-start.30
  1214.2 14.8 collective-permute-start.31
  1233.3 4.9 collective-permute-start.33
  1238.5 13.4 collective-permute-start.34
  1241.9 14.8 collective-permute-start.35
  1404.1 11.7 collective-permute-start.38
  1405.7 14.8 collective-permute-start.39
  (33 other events, 769.5 us)
where the time goes:
time: 1500 us
  blocking collectives  603 us (40%)
  local copies, waits for them, and re-layouts  561 us (37%)
  waiting for transfers between devices  143 us (10%)
  starting transfers between devices  101 us (7%)
  other arithmetic  73.8 us (5%)
    gather x3, local copies, waits for them, and re-layouts, surface_flux(): values = flat[coupling_patch_locator]  542 us
    psum x6, blocking collectives, preconditioned_product(): return lax.psum(jnp.sum(leftover_error_vector * scaled), ('px', 'py'))  398 us
    psum x3, blocking collectives, curvature_product(): return lax.psum(jnp.sum(axis_direction * image), ('px', 'py'))  205 us
    ppermute x20, waiting for transfers between devices, extended(): lax.ppermute(lax.slice_in_dim(block, block.shape[dim] - width, None, axis...  69.6 us
    ppermute x20, waiting for transfers between devices, extended(): lax.ppermute(lax.slice_in_dim(block, 0, width, axis=dim), axis, backward)  63.4 us
    ppermute x20, starting transfers between devices, extended(): lax.ppermute(lax.slice_in_dim(block, block.shape[dim] - width, None, axis...  49.7 us
  transfers between devices with their start and end apart: 43, of which 25 were waited for; matrix products, arithmetic and copies ran while one was open for 27% of the time, Pallas kernels for 0%

commit v1 on v0

--- a/solution.py
+++ b/solution.py
@@ -1,9 +1,24 @@
+import functools
+
 import jax
 import jax.numpy as jnp
 from jax import lax
+from jax.experimental import pallas as pl
+from jax.experimental.pallas import tpu as pltpu
 from jax.sharding import PartitionSpec as P
 
 ITERS = 2
+MESH = pl.DeviceIdType.MESH
+
+NZ = 24
+NX = 32
+NY = 128
+NPX = 8
+NPY = 16
+BR = 16
+STEPS = 3
+CORR = 8
+NMOM = 5
 
 
 through_ratio = 0.5
@@ -55,32 +70,28 @@
     return jnp.sum(coupling_share_factor * values, axis=0)
 
 
-def preconditioned_product(leftover_error_vector, scaled):
-    return lax.psum(jnp.sum(leftover_error_vector * scaled), ("px", "py"))
-
-
-def curvature_product(axis_direction, image):
-    return lax.psum(jnp.sum(axis_direction * image), ("px", "py"))
-
-
-def solve_step(solution, leftover_error_vector, faces, diagonal, apply, mask):
-    scaled = mask * (leftover_error_vector / diagonal)
+def total(a, b):
+    return lax.psum(jnp.sum(a * b), ("px", "py"))
+
+
+def solve_step(solution, leftover_error_vector, faces, diagonal):
+    scaled = leftover_error_vector / diagonal
     axis_direction = scaled
-    gamma = preconditioned_product(leftover_error_vector, scaled)
+    gamma = total(leftover_error_vector, scaled)
     for turn in range(ITERS):
-        image = apply(axis_direction, faces, diagonal)
-        alpha = gamma / curvature_product(axis_direction, image)
+        image = operate(axis_direction, faces, diagonal)
+        alpha = gamma / total(axis_direction, image)
         solution = solution + alpha * axis_direction
         leftover_error_vector = leftover_error_vector - alpha * image
         if turn + 1 < ITERS:
-            scaled = mask * (leftover_error_vector / diagonal)
-            fresh = preconditioned_product(leftover_error_vector, scaled)
+            scaled = leftover_error_vector / diagonal
+            fresh = total(leftover_error_vector, scaled)
             axis_direction = scaled + fresh / gamma * axis_direction
             gamma = fresh
     return (solution, leftover_error_vector)
 
 
-def body(
+def general(
     incident_power_density,
     coupling_patch_locator,
     coupling_share_factor,
@@ -93,7 +104,6 @@
     padded = jnp.pad(rimmed, ((1, 1), (0, 0), (0, 0)))
     faces = face_terms(diffusive_coefficient, padded)
     diagonal = thermal_storage + faces[0] + faces[1] + faces[2] + faces[3] + faces[4] + faces[5]
-    mask = jnp.ones((1, 1, 1), jnp.float32)
     frames = incident_power_density.shape[0]
     final_warmth = starting_warmth
     leftover_error_vector = starting_warmth
@@ -102,14 +112,625 @@
             incident_power_density[frame : frame + 1], "py", split_axis=2, concat_axis=1, tiled=True
         )[0]
         flux = surface_flux(window, coupling_patch_locator, coupling_share_factor)
-        solution = final_warmth
         right = thermal_storage * final_warmth
         right = right.at[sheet_level - 1].add(flux)
-        leftover_error_vector = right - operate(solution, faces, diagonal)
+        leftover_error_vector = right - operate(final_warmth, faces, diagonal)
         final_warmth, leftover_error_vector = solve_step(
-            solution, leftover_error_vector, faces, diagonal, operate, mask
+            final_warmth, leftover_error_vector, faces, diagonal
         )
     return (final_warmth, leftover_error_vector)
+
+
+def lanes(rows=NZ):
+    return lax.broadcasted_iota(jnp.int32, (rows, NY), 1)
+
+
+def rolled(v, shift, axis=1):
+    return pltpu.roll(v, shift % v.shape[axis], axis)
+
+
+def side_tile(packed, x):
+    return pltpu.roll(packed, lax.rem(638 - 4 * x, 128), 1)
+
+
+def lateral(v, side):
+    lane = lanes(v.shape[0])
+    left = jnp.where(lane == 0, side, rolled(v, 1))
+    right = jnp.where(lane == NY - 1, side, rolled(v, -1))
+    return left, right
+
+
+def apply_slab(ref, i, side, g_ref, gi):
+    v = ref[i]
+    left, right = lateral(v, side)
+    out = g_ref[0, gi] * rolled(v, 1, 0) + g_ref[1, gi] * rolled(v, -1, 0)
+    out = out + (g_ref[2, gi] * ref[i - 1] + g_ref[3, gi] * ref[i + 1])
+    out = out + (g_ref[4, gi] * left + g_ref[5, gi] * right)
+    return v - out
+
+
+def around_halo(halo, corner, pack):
+    lane = lanes()
+    j = lax.rem(lane, 4)
+    below = jnp.where(lane < 4, corner, rolled(halo, 4))
+    above = jnp.where(lane >= NY - 4, corner, rolled(halo, -4))
+    outer = jnp.where(j == 1, rolled(halo, 1), rolled(halo, -1))
+    return below, above, pack, outer
+
+
+def apply_halo(halo, corner, pack, gp_ref):
+    below, above, inner, outer = around_halo(halo, corner, pack)
+    out = gp_ref[0] * rolled(halo, 1, 0) + gp_ref[1] * rolled(halo, -1, 0)
+    out = out + gp_ref[2] * below + gp_ref[3] * above + gp_ref[4] * inner + gp_ref[5] * outer
+    return halo - out
+
+
+class Place:
+    def __init__(self):
+        self.px = lax.axis_index("px")
+        self.py = lax.axis_index("py")
+        self.has_low = jnp.where(self.px > 0, 1.0, 0.0).astype(jnp.float32)
+        self.has_high = jnp.where(self.px < NPX - 1, 1.0, 0.0).astype(jnp.float32)
+        self.has_left = jnp.where(self.py > 0, 1.0, 0.0).astype(jnp.float32)
+        self.has_right = jnp.where(self.py < NPY - 1, 1.0, 0.0).astype(jnp.float32)
+
+    def at(self, dx, dy):
+        return (lax.rem(self.px + dx + NPX, NPX), lax.rem(self.py + dy + NPY, NPY))
+
+
+CORNERS = ((-1, 1), (-1, -1), (1, 1), (1, -1))
+
+
+class Exchange:
+    def __init__(self, place, refs):
+        self.place = place
+        self.rx, self.rs, self.rk, self.pack, self.send, self.recv = refs
+        self.copies = []
+
+    def start(self, low, high):
+        place = self.place
+        plan = []
+        for n, (dx, dy) in enumerate(CORNERS):
+            plan.append((self.pack, self.rk.at[n], (-dx, -dy)))
+        plan.append((self.pack, self.rs.at[0], (0, 1)))
+        plan.append((self.pack, self.rs.at[1], (0, -1)))
+        single = len(low.shape) == 3
+        for n, (src, dx) in enumerate(((high, 1), (low, -1))):
+            plan.append((src, self.rx.at[n, 0] if single else self.rx.at[n], (dx, 0)))
+        for n, (src, dst, (dx, dy)) in enumerate(plan):
+            copy = pltpu.make_async_remote_copy(
+                src_ref=src,
+                dst_ref=dst,
+                send_sem=self.send.at[n],
+                recv_sem=self.recv.at[n],
+                device_id=place.at(dx, dy),
+                device_id_type=MESH,
+            )
+            copy.start()
+            self.copies.append(copy)
+
+    def arrive(self):
+        for copy in self.copies:
+            copy.wait_recv()
+
+    def sent(self):
+        for copy in self.copies:
+            copy.wait_send()
+
+    def slabs(self, field):
+        p = self.place
+        return (
+            self.rx[0, field, 0] * p.has_low,
+            self.rx[0, field, 1] * p.has_low,
+            self.rx[1, field, 0] * p.has_high,
+            self.rx[1, field, 1] * p.has_high,
+        )
+
+    def halo(self, field):
+        p = self.place
+        left = self.rs[0, field] * p.has_left
+        right = self.rs[1, field] * p.has_right
+        j = lax.rem(lanes(left.shape[0]), 4)
+        far = jnp.where(j == 0, rolled(right, -3), rolled(left, 3))
+        near = jnp.where(j == 1, rolled(right, -1), rolled(left, 1))
+        return jnp.where((j == 1) | (j == 2), near, far)
+
+    def corner(self, field):
+        p = self.place
+        a = rolled(self.rk[0, field] * (p.has_low * p.has_right), 3)
+        b = rolled(self.rk[1, field] * (p.has_low * p.has_left), 5)
+        c = rolled(self.rk[2, field] * (p.has_high * p.has_right), -5)
+        d = rolled(self.rk[3, field] * (p.has_high * p.has_left), -3)
+        lane = lanes(a.shape[0])
+        out = jnp.where(lane == 1, a, jnp.zeros_like(a))
+        out = jnp.where(lane == 2, b, out)
+        out = jnp.where(lane == NY - 3, c, out)
+        return jnp.where(lane == NY - 2, d, out)
+
+
+def packed_into(pack, v, x):
+    lane = lanes(v.shape[0])
+    return jnp.where(lane // 4 == x, pltpu.roll(v, lax.rem(4 * x + 2, NY), 1), pack)
+
+
+HOPS = sorted(
+    ((dz, dy) for dz in range(4) for dy in range(4) if dz or dy),
+    key=lambda t: -(min(t[0], 4 - t[0]) + min(t[1], 4 - t[1])),
+)
+
+
+def ring_targets(place):
+    x, core = place.px // 2, lax.rem(place.px, 2)
+    z, y = place.py // 4, lax.rem(place.py, 4)
+    px = []
+    for dx, dc in ((2, 1), (2, 0), (1, 1), (1, 0), (3, 1), (3, 0), (0, 1)):
+        px.append((lax.rem(x + dx, 4) * 2 + lax.rem(core + dc, 2), place.py))
+    py = []
+    for dz, dy in HOPS:
+        py.append((place.px, lax.rem(z + dz, 4) * 4 + lax.rem(y + dy, 4)))
+    return px, py
+
+
+def kernel(
+    beam,
+    loc_in,
+    share_in,
+    t_in,
+    k_in,
+    c_in,
+    x_out,
+    r_out,
+    flag_out,
+    kraw,
+    craw,
+    traw,
+    loc,
+    share,
+    window,
+    weights,
+    kct,
+    z_ref,
+    u_ref,
+    v_ref,
+    x_ref,
+    g_ref,
+    gp_ref,
+    d_ref,
+    e_ref,
+    fd_ref,
+    red_src,
+    red_px,
+    red_py,
+    local_sem,
+    beam_send,
+    beam_recv,
+    red_send,
+    red_recv,
+    *exchange_refs,
+):
+    place = Place()
+    px_ring, py_ring = ring_targets(place)
+    diagonal_devices = [place.at(dx, dy) for dx, dy in CORNERS]
+
+    local = [
+        pltpu.make_async_copy(src, dst, local_sem.at[n])
+        for n, (src, dst) in enumerate(
+            (
+                (k_in, kraw),
+                (c_in, craw),
+                (t_in, traw),
+                (loc_in, loc),
+                (share_in, share),
+            )
+        )
+    ]
+    for copy in local:
+        copy.start()
+    own_columns = pl.ds(pl.multiple_of(place.py * NY, NY), NY)
+    own_rows = pl.ds(pl.multiple_of(place.py * BR, BR), BR)
+    own_beam = pltpu.make_async_copy(
+        beam.at[:, :, own_columns], window.at[:, own_rows, :], local_sem.at[5]
+    )
+    own_beam.start()
+
+    barrier = pltpu.get_barrier_semaphore()
+    everyone = py_ring + px_ring + diagonal_devices
+    for device in everyone:
+        pl.semaphore_signal(barrier, inc=1, device_id=device, device_id_type=MESH)
+
+    exchanges = [
+        Exchange(place, exchange_refs[6 * n : 6 * n + 6]) for n in range(1 + STEPS)
+    ]
+
+    for copy in local[:3]:
+        copy.wait()
+    zero = jnp.zeros((NZ, NY), jnp.float32)
+
+    def lay(x, packs):
+        out = []
+        for n, raw in enumerate((kraw, craw, traw)):
+            v = raw[pl.ds(x, NZ, stride=NX), :]
+            kct[n, x + 2] = v
+            out.append(packed_into(packs[n], v, x))
+        return tuple(out)
+
+    packs = lax.fori_loop(0, NX, lay, (zero, zero, zero))
+    k_pack, c_pack, t_pack = packs
+    first = exchanges[0]
+    for n in range(3):
+        first.pack[n] = packs[n]
+
+    pl.semaphore_wait(barrier, len(everyone))
+
+    def send_frame(frame):
+        copies = []
+        for device in py_ring:
+            columns = pl.ds(pl.multiple_of(device[1] * NY, NY), NY)
+            copy = pltpu.make_async_remote_copy(
+                src_ref=beam.at[frame, :, columns],
+                dst_ref=window.at[frame, own_rows, :],
+                send_sem=beam_send.at[frame],
+                recv_sem=beam_recv.at[frame],
+                device_id=device,
+                device_id_type=MESH,
+            )
+            copy.start()
+
+    def frame_bytes(frame, sem):
+        most = window.at[frame, pl.ds(0, (NPY - 1) * BR), :]
+        return pltpu.make_async_copy(most, most, sem.at[frame])
+
+    send_frame(0)
+    first.start(kct.at[:, 2:4], kct.at[:, NX : NX + 2])
+    for frame in range(1, STEPS):
+        send_frame(frame)
+
+    local[3].wait()
+    local[4].wait()
+    row8 = lax.broadcasted_iota(jnp.int32, (8, NY), 0)
+    lane8 = lax.broadcasted_iota(jnp.int32, (8, NY), 1)
+    beyond = jnp.where(row8 == 7, -1, jnp.where(row8 == 0, 8, -1000))
+
+    def weigh(x, bad):
+        own = [jnp.zeros((8, NY), jnp.float32) for _ in range(3)]
+        edge = [jnp.zeros((8, NY), jnp.float32) for _ in range(3)]
+        for k in range(CORR):
+            index = jnp.broadcast_to(loc[k, pl.ds(x, 1), :], (8, NY))
+            part = jnp.broadcast_to(share[k, pl.ds(x, 1), :], (8, NY))
+            row = lax.shift_right_arithmetic(index, 7) - 8 * x
+            col = lax.bitwise_and(index, 127) - lane8
+            far = (row < -1) | (row > 8) | (col < -1) | (col > 1)
+            bad = bad + jnp.where(far, 1.0, 0.0)
+            inside = jnp.where(row == row8, part, 0.0)
+            outside = jnp.where(row == beyond, part, 0.0)
+            for n in range(3):
+                here = col == n - 1
+                own[n] = own[n] + jnp.where(here, inside, 0.0)
+                edge[n] = edge[n] + jnp.where(here, outside, 0.0)
+        for n in range(3):
+            weights[n, x] = own[n]
+            weights[3 + n, x] = edge[n]
+        return bad
+
+    bad = lax.fori_loop(0, NX, weigh, jnp.zeros((8, NY), jnp.float32))
+
+    first.arrive()
+    for n in range(3):
+        slabs = first.slabs(n)
+        for at, slab in zip((0, 1, NX + 2, NX + 3), slabs):
+            kct[n, at] = slab
+    k_halo, k_corner = first.halo(0), first.corner(0)
+    c_halo, t_halo = first.halo(1), first.halo(2)
+    level = lax.broadcasted_iota(jnp.int32, (NZ, NY), 0)
+
+    def over(k, up, down, below, above, left, right, storage, mask):
+        bottom, top = level == 0, level == NZ - 1
+        up = jnp.where(bottom, 0.0, up)
+        down = jnp.where(top, 0.0, down)
+        faces = [0.25 * (k + up), 0.25 * (k + down)]
+        faces += [0.5 * (k + other) for other in (below, above, left, right)]
+        diagonal = storage + (
+            (faces[0] + faces[1]) + (faces[2] + faces[3]) + (faces[4] + faces[5])
+        )
+        inverse = mask / diagonal
+        faces[0] = jnp.where(bottom, 0.0, faces[0])
+        faces[1] = jnp.where(top, 0.0, faces[1])
+        return [face * inverse for face in faces], diagonal, inverse
+
+    def conduct(x, side, mask):
+        i = x + 2
+        k = kct[0, i]
+        left, right = lateral(k, side)
+        g, diagonal, inverse = over(
+            k,
+            rolled(k, 1, 0),
+            rolled(k, -1, 0),
+            kct[0, i - 1],
+            kct[0, i + 1],
+            left,
+            right,
+            kct[1, i],
+            mask,
+        )
+        for n in range(6):
+            g_ref[n, x + 1] = g[n]
+        return diagonal, inverse
+
+    conduct(-1, side_tile(k_corner, 0), place.has_low)
+    conduct(NX, side_tile(k_corner, NX - 1), place.has_high)
+
+    def conduct_inside(x, carry):
+        diagonal, inverse = conduct(x, side_tile(k_halo, x), 1.0)
+        d_ref[x] = diagonal
+        e_ref[x] = kct[1, x + 2] * inverse
+        return carry
+
+    lax.fori_loop(0, NX, conduct_inside, 0)
+
+    below, above, inner, outer = around_halo(k_halo, k_corner, k_pack)
+    j = lax.rem(lanes(), 4)
+    halo_mask = jnp.where(j < 2, place.has_right, place.has_left)
+    halo_mask = jnp.where((j == 1) | (j == 2), halo_mask, 0.0)
+    gp, _, _ = over(
+        k_halo,
+        rolled(k_halo, 1, 0),
+        rolled(k_halo, -1, 0),
+        below,
+        above,
+        inner,
+        outer,
+        c_halo + jnp.where(halo_mask > 0.0, 0.0, 1.0),
+        halo_mask,
+    )
+    for n in range(6):
+        gp_ref[n] = gp[n]
+
+    t_ref = kct.at[2]
+
+    def residual(x, carry):
+        image = apply_slab(t_ref, x + 2, side_tile(t_halo, x), g_ref, x + 1)
+        t = t_ref[x + 2]
+        z_ref[x + 2] = e_ref[x] * t - image
+        x_ref[x] = t
+        return carry
+
+    lax.fori_loop(0, NX, residual, 0)
+    first.sent()
+
+    own_beam.wait()
+
+    def flux_tile(frame, x):
+        def rows(i):
+            return window[frame, pl.ds(pl.multiple_of(i * 8, 8), 8), :]
+
+        mine = rows(x)
+        around = jnp.where(
+            row8 == 7, rows(jnp.maximum(x - 1, 0)), rows(jnp.minimum(x + 1, NX - 1))
+        )
+        part = weights[1, x] * mine + weights[4, x] * around
+        part = part + weights[0, x] * rolled(mine, 1) + weights[3, x] * rolled(around, 1)
+        part = part + weights[2, x] * rolled(mine, -1) + weights[5, x] * rolled(around, -1)
+        flux = jnp.sum(part, axis=0, keepdims=True)
+        top = d_ref[x, NZ - 8 : NZ, :]
+        return jnp.where(row8 == 7, flux, 0.0) / top
+
+    def zero_row():
+        return jnp.zeros((8, NY), jnp.float32)
+
+    def all_sum(step, moments):
+        lane = lax.broadcasted_iota(jnp.int32, (1, NY), 1)
+        row = jnp.zeros((1, NY), jnp.float32)
+        for n, m in enumerate(moments):
+            row = jnp.where(lane == n, jnp.sum(m, keepdims=True), row)
+        for phase, (ring, slots, me) in enumerate(
+            ((px_ring, red_px, place.px), (py_ring, red_py, place.py))
+        ):
+            source = red_src.at[step, phase]
+            source[...] = row
+            for device in ring:
+                pltpu.make_async_remote_copy(
+                    src_ref=source,
+                    dst_ref=slots.at[step, me],
+                    send_sem=red_send.at[step, phase],
+                    recv_sem=red_recv.at[step, phase],
+                    device_id=device,
+                    device_id_type=MESH,
+                ).start()
+            slots[step, me] = row
+            most = slots.at[step, pl.ds(0, len(ring))]
+            pltpu.make_async_copy(most, most, red_recv.at[step, phase]).wait()
+            parts = [slots[step, n] for n in range(len(ring) + 1)]
+            while len(parts) > 1:
+                parts = [a + b for a, b in zip(parts[::2], parts[1::2])]
+            row = parts[0]
+        return [
+            jnp.sum(jnp.where(lane == n, row, 0.0), axis=1, keepdims=True)
+            for n in range(len(moments))
+        ]
+
+    def folded(v):
+        return v[0:8] + v[8:16] + v[16:24]
+
+    for step in range(STEPS):
+        exchange = exchanges[1 + step]
+        if step == 0:
+            frame_bytes(0, beam_recv).wait()
+
+            def add_flux(x, pack):
+                tile = flux_tile(0, x)
+                fd_ref[0, x] = tile
+                z_ref[x + 2, NZ - 8 : NZ, :] = z_ref[x + 2, NZ - 8 : NZ, :] + tile
+                return packed_into(pack, z_ref[x + 2], x)
+
+            z_pack = lax.fori_loop(0, NX, add_flux, zero)
+        exchange.pack[0] = z_pack
+        exchange.start(z_ref.at[pl.ds(2, 2)], z_ref.at[pl.ds(NX, 2)])
+        if step + 1 < STEPS:
+            frame_bytes(step + 1, beam_recv).wait()
+
+            def next_flux(x, carry):
+                fd_ref[step + 1, x] = flux_tile(step + 1, x)
+                return carry
+
+            lax.fori_loop(0, NX, next_flux, 0)
+        exchange.arrive()
+        slabs = exchange.slabs(0)
+        for at, slab in zip((0, 1, NX + 2, NX + 3), slabs):
+            z_ref[at] = slab
+        z_halo, z_corner = exchange.halo(0), exchange.corner(0)
+
+        u_ref[1] = apply_slab(z_ref, 1, side_tile(z_corner, 0), g_ref, 0)
+        u_ref[NX + 2] = apply_slab(z_ref, NX + 2, side_tile(z_corner, NX - 1), g_ref, NX + 1)
+        u_halo = apply_halo(z_halo, z_corner, z_pack, gp_ref)
+
+        def first_image(x, sums):
+            u = apply_slab(z_ref, x + 2, side_tile(z_halo, x), g_ref, x + 1)
+            u_ref[x + 2] = u
+            z = z_ref[x + 2]
+            dz = d_ref[x] * z
+            du = d_ref[x] * u
+            return (
+                sums[0] + folded(dz * z),
+                sums[1] + folded(dz * u),
+                sums[2] + folded(du * u),
+            )
+
+        sums = lax.fori_loop(0, NX, first_image, (zero_row(),) * 3)
+
+        def second_image(x, acc):
+            v = apply_slab(u_ref, x + 2, side_tile(u_halo, x), g_ref, x + 1)
+            v_ref[x] = v
+            return acc + folded(d_ref[x] * u_ref[x + 2] * v)
+
+        last = lax.fori_loop(0, NX, second_image, zero_row())
+        g0, a, w, t, *rest = all_sum(step, list(sums) + [last] + ([bad] if step == 0 else []))
+        if step == 0:
+            flag_out[...] = jnp.broadcast_to(rest[0], (8, NY))
+        alpha0 = g0 / a
+        gamma1 = alpha0 * alpha0 * w - g0
+        beta1 = 1.0 + gamma1 / g0
+        alpha1 = gamma1 / (beta1 * beta1 * a - 2.0 * beta1 * alpha0 * w + alpha0 * alpha0 * t)
+        d1 = jnp.broadcast_to(alpha0 + alpha1 * beta1, (NZ, NY))
+        d2 = jnp.broadcast_to(-alpha0 * alpha1, (NZ, NY))
+        exchange.sent()
+
+        if step + 1 < STEPS:
+
+            def update(x, pack):
+                z, u, v = z_ref[x + 2], u_ref[x + 2], v_ref[x]
+                move = d1 * z + d2 * u
+                x_ref[x] = x_ref[x] + move
+                z_ref[x + 2] = z - d1 * u - d2 * v + e_ref[x] * move
+                tile = fd_ref[step + 1, x] - fd_ref[step, x]
+                z_ref[x + 2, NZ - 8 : NZ, :] = z_ref[x + 2, NZ - 8 : NZ, :] + tile
+                return packed_into(pack, z_ref[x + 2], x)
+
+            z_pack = lax.fori_loop(0, NX, update, zero)
+        else:
+
+            def finish(x, carry):
+                z, u, v = z_ref[x + 2], u_ref[x + 2], v_ref[x]
+                x_out[pl.ds(x, NZ, stride=NX), :] = x_ref[x] + (d1 * z + d2 * u)
+                r_out[pl.ds(x, NZ, stride=NX), :] = d_ref[x] * (z - d1 * u - d2 * v)
+                return carry
+
+            lax.fori_loop(0, NX, finish, 0)
+
+    for frame in range(STEPS):
+        frame_bytes(frame, beam_send).wait()
+    for step in range(STEPS):
+        for phase, (slots, count) in enumerate(((red_px, NPX - 1), (red_py, NPY - 1))):
+            most = slots.at[step, pl.ds(0, count)]
+            pltpu.make_async_copy(most, most, red_send.at[step, phase]).wait()
+
+
+def exchange_scratch(fields, rows=NZ):
+    f32 = jnp.float32
+    return [
+        pltpu.VMEM((2, fields, 2, rows, NY), f32),
+        pltpu.VMEM((2, fields, rows, NY), f32),
+        pltpu.VMEM((4, fields, rows, NY), f32),
+        pltpu.VMEM((fields, rows, NY), f32),
+        pltpu.SemaphoreType.DMA((8,)),
+        pltpu.SemaphoreType.DMA((8,)),
+    ]
+
+
+def body(
+    incident_power_density,
+    coupling_patch_locator,
+    coupling_share_factor,
+    starting_warmth,
+    diffusive_coefficient,
+    thermal_storage,
+):
+    f32 = jnp.float32
+    flat = (NZ * NX, NY)
+    hbm = pl.BlockSpec(memory_space=pl.ANY)
+    vmem = pl.BlockSpec(memory_space=pltpu.VMEM)
+    scratch = [
+        pltpu.VMEM(flat, f32),
+        pltpu.VMEM(flat, f32),
+        pltpu.VMEM(flat, f32),
+        pltpu.VMEM((CORR, NX, NY), jnp.int32),
+        pltpu.VMEM((CORR, NX, NY), f32),
+        pltpu.VMEM((STEPS, BR * NPY, NY), f32),
+        pltpu.VMEM((6, NX, 8, NY), f32),
+        pltpu.VMEM((3, NX + 4, NZ, NY), f32),
+        pltpu.VMEM((NX + 4, NZ, NY), f32),
+        pltpu.VMEM((NX + 4, NZ, NY), f32),
+        pltpu.VMEM((NX, NZ, NY), f32),
+        pltpu.VMEM((NX, NZ, NY), f32),
+        pltpu.VMEM((6, NX + 2, NZ, NY), f32),
+        pltpu.VMEM((6, NZ, NY), f32),
+        pltpu.VMEM((NX, NZ, NY), f32),
+        pltpu.VMEM((NX, NZ, NY), f32),
+        pltpu.VMEM((STEPS, NX, 8, NY), f32),
+        pltpu.VMEM((STEPS, 2, 1, NY), f32),
+        pltpu.VMEM((STEPS, NPX, 1, NY), f32),
+        pltpu.VMEM((STEPS, NPY, 1, NY), f32),
+        pltpu.SemaphoreType.DMA((6,)),
+        pltpu.SemaphoreType.DMA((STEPS,)),
+        pltpu.SemaphoreType.DMA((STEPS,)),
+        pltpu.SemaphoreType.DMA((STEPS, 2)),
+        pltpu.SemaphoreType.DMA((STEPS, 2)),
+    ]
+    for fields in (3, 1, 1, 1):
+        scratch += exchange_scratch(fields)
+    warmth, leftover, flag = pl.pallas_call(
+        kernel,
+        out_shape=(
+            jax.ShapeDtypeStruct(flat, f32),
+            jax.ShapeDtypeStruct(flat, f32),
+            jax.ShapeDtypeStruct((8, NY), f32),
+        ),
+        in_specs=[hbm] * 6,
+        out_specs=(vmem, vmem, vmem),
+        scratch_shapes=scratch,
+        compiler_params=pltpu.CompilerParams(
+            collective_id=0, has_side_effects=True, vmem_limit_bytes=40 * 2**20
+        ),
+    )(
+        incident_power_density,
+        coupling_patch_locator,
+        coupling_share_factor,
+        starting_warmth.reshape(flat),
+        diffusive_coefficient.reshape(flat),
+        thermal_storage.reshape(flat),
+    )
+    shape = starting_warmth.shape
+    return lax.cond(
+        flag[0, 0] > 0.0,
+        lambda: general(
+            incident_power_density,
+            coupling_patch_locator,
+            coupling_share_factor,
+            starting_warmth,
+            diffusive_coefficient,
+            thermal_storage,
+        ),
+        lambda: (warmth.reshape(shape), leftover.reshape(shape)),
+    )
 
 
 def solution(mesh):

time: 1500 us -> 96.6 us (0.06)
  blocking collectives: 603 us -> 0 us
  local copies, waits for them, and re-layouts: 561 us -> 4.07 us
  waiting for transfers between devices: 143 us -> 0 us
  starting transfers between devices: 101 us -> 0 us
  Pallas kernels: 0 us -> 90.7 us
  other arithmetic: 73.8 us -> 0 us
    psum x9 -> x0, blocking collectives: 603 us -> none  [the longest x6 398 us: preconditioned_product(): return lax.psum(jnp.sum(leftover_error_vector * scaled), ('px', 'py'))]
    gather x3 -> x0, local copies, waits for them, and re-layouts: 542 us -> none  [surface_flux(): values = flat[coupling_patch_locator]]
    ppermute x40 -> x0, waiting for transfers between devices: 133 us -> none  [the longest x20 69.6 us: extended(): lax.ppermute(lax.slice_in_dim(block, block.shape[dim] - width, None, axis...]
    pallas_call x0 -> x1, Pallas kernels: none -> 90.7 us  [body(): pl.pallas_call(kernel, out_shape=(jax.ShapeDtypeStruct(flat, f32), jax.Sh...]
    ppermute x40 -> x0, starting transfers between devices: 75.8 us -> none  [the longest x20 49.7 us: extended(): lax.ppermute(lax.slice_in_dim(block, block.shape[dim] - width, None, axis...]
    unnamed x3 -> x0, other arithmetic: 27.9 us -> none
    all_to_all x3 -> x0, starting transfers between devices: 25.1 us -> none  [body(): lax.all_to_all(incident_power_density[frame:frame + 1], 'py', split_axis=...]
    reduce_sum x10 -> x0, other arithmetic: 18.1 us -> none  [the longest x6 11.3 us: curvature_product(): return lax.psum(jnp.sum(axis_direction * image), ('px', 'py'))]
  transfers between devices with their start and end apart: 43 -> 0, of which waited for: 25 -> 0; matrix products, arithmetic and copies ran while one was open for 27% -> 0% of each run, Pallas kernels for 0% -> 0%
where the time goes in v1:
time: 96.6 us; the launch traced here: 96.4 us
  Pallas kernels  90.7 us (94%)
  local copies, waits for them, and re-layouts  4.07 us (4%)
  between operations  1.4 us (1%)
    pallas_call x1, Pallas kernels, body(): pl.pallas_call(kernel, out_shape=(jax.ShapeDtypeStruct(flat, f32), jax.Sh...  90.7 us
    unnamed x14, local copies, waits for them, and re-layouts  3.56 us

profile of v1, /device:TPU:0, one launch (start us, length us, event | category | flops | bytes accessed | tf_op | source)
XLA Modules:
  0.0 96.4 jit_solution(5885361188474462050)
XLA Ops:
  0.6 0.0 copy-start.10
  0.6 0.0 copy-start.18
  0.7 0.0 copy-start.19
  0.7 0.0 copy-start.1
  0.7 0.0 copy-start
  0.7 0.0 copy-start.3
  0.7 90.7 %shard_map.81 = (f32[768,128]{1,0:T(8,128)}, f32[768,128]{1,0:T(8,128)}, f32[8,128]{1,0:T(8,128)S(1)}) custom-call(f32[3,16,2048]{2,1,0:T(8,128)} %beam.1, s32[8,32,128]{2,1,0:T(8,128)} %loc_in.1, f32[8,32,128]{2,1,0:T(8,128)} %share_in.1, f32[768,128]{1,0:T(8,128)} %bitcast.38, f32[768,128]{1,0:T(8,128)} %bitcast.37, f32[768,128]{1,0:T(8,128)} %bitcast.39), custom_call_target="tpu_custom_call" | custom-call | tf_op jit(solution)/shard_map/pallas_call | solution.py:700
  91.4 0.5 slice.478
  92.6 0.0 copy-done.10
  92.6 0.0 copy-done.18
  92.6 0.0 copy-done.19
  92.6 0.0 copy-done.1
  92.6 0.0 copy-done
  92.6 0.0 copy-done.3
  92.6 0.2 conditional.1
  92.9 1.8 %copy.39 = f32[24,32,128]{2,1,0:T(8,128)} copy(f32[24,32,128]{2,1,0:T(8,128)} %get-tuple-element.177) | data formatting | bytes 786432
  94.6 1.8 %copy.40 = f32[24,32,128]{2,1,0:T(8,128)} copy(f32[24,32,128]{2,1,0:T(8,128)} %get-tuple-element.178) | data formatting | bytes 786432
Async XLA Ops:
  0.6 92.0 %copy-start.10 = (f32[3,16,2048]{2,1,0:T(8,128)S(1)}, f32[3,16,2048]{2,1,0:T(8,128)}, u32[]{:S(2)}) copy-start(f32[3,16,2048]{2,1,0:T(8,128)} %beam.1) | copy-start | bytes 1179652
  0.6 92.0 %copy-start.18 = (s32[8,32,128]{2,1,0:T(8,128)S(1)}, s32[8,32,128]{2,1,0:T(8,128)}, u32[]{:S(2)}) copy-start(s32[8,32,128]{2,1,0:T(8,128)} %loc_in.1) | copy-start | bytes 393220
  0.7 92.0 %copy-start.19 = (f32[8,32,128]{2,1,0:T(8,128)S(1)}, f32[8,32,128]{2,1,0:T(8,128)}, u32[]{:S(2)}) copy-start(f32[8,32,128]{2,1,0:T(8,128)} %share_in.1) | copy-start | bytes 393220
  0.7 92.0 %copy-start.1 = (f32[24,32,128]{2,1,0:T(8,128)S(1)}, f32[24,32,128]{2,1,0:T(8,128)}, u32[]{:S(2)}) copy-start(f32[24,32,128]{2,1,0:T(8,128)} %param.17) | copy-start | bytes 1179652
  0.7 92.0 %copy-start = (f32[24,32,128]{2,1,0:T(8,128)S(1)}, f32[24,32,128]{2,1,0:T(8,128)}, u32[]{:S(2)}) copy-start(f32[24,32,128]{2,1,0:T(8,128)} %param.18) | copy-start | bytes 1179652
  0.7 92.0 %copy-start.3 = (f32[24,32,128]{2,1,0:T(8,128)S(1)}, f32[24,32,128]{2,1,0:T(8,128)}, u32[]{:S(2)}) copy-start(f32[24,32,128]{2,1,0:T(8,128)} %param.19) | copy-start | bytes 1179652

commit v2 on v1

--- a/solution.py
+++ b/solution.py
@@ -18,7 +18,7 @@
 BR = 16
 STEPS = 3
 CORR = 8
-NMOM = 5
+UNROLL = 8
 
 
 through_ratio = 0.5
@@ -129,6 +129,15 @@
     return pltpu.roll(v, shift % v.shape[axis], axis)
 
 
+def slabs_loop(fn, init, step=UNROLL):
+    def some(n, carry):
+        for q in range(step):
+            carry = fn(n * step + q, carry)
+        return carry
+
+    return lax.fori_loop(0, NX // step, some, init)
+
+
 def side_tile(packed, x):
     return pltpu.roll(packed, lax.rem(638 - 4 * x, 128), 1)
 
@@ -178,6 +187,8 @@
         return (lax.rem(self.px + dx + NPX, NPX), lax.rem(self.py + dy + NPY, NPY))
 
 
+GHOSTS = (0, 1, NX + 2, NX + 3)
+EXCHANGES = ((3, NZ), (1, NZ), (1, NZ), (2, 8), (2, NZ), (2, NZ))
 CORNERS = ((-1, 1), (-1, -1), (1, 1), (1, -1))
 
 
@@ -290,8 +301,7 @@
     weights,
     kct,
     z_ref,
-    u_ref,
-    v_ref,
+    uv_ref,
     x_ref,
     g_ref,
     gp_ref,
@@ -309,6 +319,7 @@
     *exchange_refs,
 ):
     place = Place()
+    u_ref, v_ref = uv_ref.at[0], uv_ref.at[1]
     px_ring, py_ring = ring_targets(place)
     diagonal_devices = [place.at(dx, dy) for dx, dy in CORNERS]
 
@@ -339,8 +350,9 @@
         pl.semaphore_signal(barrier, inc=1, device_id=device, device_id_type=MESH)
 
     exchanges = [
-        Exchange(place, exchange_refs[6 * n : 6 * n + 6]) for n in range(1 + STEPS)
+        Exchange(place, exchange_refs[6 * n : 6 * n + 6]) for n in range(len(EXCHANGES))
     ]
+    first, z_swap, e_swap, f_swap, *uv_swaps = exchanges
 
     for copy in local[:3]:
         copy.wait()
@@ -354,36 +366,10 @@
             out.append(packed_into(packs[n], v, x))
         return tuple(out)
 
-    packs = lax.fori_loop(0, NX, lay, (zero, zero, zero))
+    packs = slabs_loop(lay, (zero, zero, zero))
     k_pack, c_pack, t_pack = packs
-    first = exchanges[0]
     for n in range(3):
         first.pack[n] = packs[n]
-
-    pl.semaphore_wait(barrier, len(everyone))
-
-    def send_frame(frame):
-        copies = []
-        for device in py_ring:
-            columns = pl.ds(pl.multiple_of(device[1] * NY, NY), NY)
-            copy = pltpu.make_async_remote_copy(
-                src_ref=beam.at[frame, :, columns],
-                dst_ref=window.at[frame, own_rows, :],
-                send_sem=beam_send.at[frame],
-                recv_sem=beam_recv.at[frame],
-                device_id=device,
-                device_id_type=MESH,
-            )
-            copy.start()
-
-    def frame_bytes(frame, sem):
-        most = window.at[frame, pl.ds(0, (NPY - 1) * BR), :]
-        return pltpu.make_async_copy(most, most, sem.at[frame])
-
-    send_frame(0)
-    first.start(kct.at[:, 2:4], kct.at[:, NX : NX + 2])
-    for frame in range(1, STEPS):
-        send_frame(frame)
 
     local[3].wait()
     local[4].wait()
@@ -412,12 +398,37 @@
             weights[3 + n, x] = edge[n]
         return bad
 
-    bad = lax.fori_loop(0, NX, weigh, jnp.zeros((8, NY), jnp.float32))
+    bad = slabs_loop(weigh, jnp.zeros((8, NY), jnp.float32))
+
+    pl.semaphore_wait(barrier, len(everyone))
+
+    def send_frame(frame):
+        copies = []
+        for device in py_ring:
+            columns = pl.ds(pl.multiple_of(device[1] * NY, NY), NY)
+            copy = pltpu.make_async_remote_copy(
+                src_ref=beam.at[frame, :, columns],
+                dst_ref=window.at[frame, own_rows, :],
+                send_sem=beam_send.at[frame],
+                recv_sem=beam_recv.at[frame],
+                device_id=device,
+                device_id_type=MESH,
+            )
+            copy.start()
+
+    def frame_bytes(frame, sem):
+        most = window.at[frame, pl.ds(0, (NPY - 1) * BR), :]
+        return pltpu.make_async_copy(most, most, sem.at[frame])
+
+    send_frame(0)
+    first.start(kct.at[:, 2:4], kct.at[:, NX : NX + 2])
+    for frame in range(1, STEPS):
+        send_frame(frame)
 
     first.arrive()
     for n in range(3):
         slabs = first.slabs(n)
-        for at, slab in zip((0, 1, NX + 2, NX + 3), slabs):
+        for at, slab in zip(GHOSTS, slabs):
             kct[n, at] = slab
     k_halo, k_corner = first.halo(0), first.corner(0)
     c_halo, t_halo = first.halo(1), first.halo(2)
@@ -459,13 +470,14 @@
     conduct(-1, side_tile(k_corner, 0), place.has_low)
     conduct(NX, side_tile(k_corner, NX - 1), place.has_high)
 
-    def conduct_inside(x, carry):
+    def conduct_inside(x, pack):
         diagonal, inverse = conduct(x, side_tile(k_halo, x), 1.0)
         d_ref[x] = diagonal
-        e_ref[x] = kct[1, x + 2] * inverse
-        return carry
-
-    lax.fori_loop(0, NX, conduct_inside, 0)
+        e = kct[1, x + 2] * inverse
+        e_ref[x + 2] = e
+        return packed_into(pack, e, x)
+
+    e_swap.pack[0] = slabs_loop(conduct_inside, zero)
 
     below, above, inner, outer = around_halo(k_halo, k_corner, k_pack)
     j = lax.rem(lanes(), 4)
@@ -490,11 +502,11 @@
     def residual(x, carry):
         image = apply_slab(t_ref, x + 2, side_tile(t_halo, x), g_ref, x + 1)
         t = t_ref[x + 2]
-        z_ref[x + 2] = e_ref[x] * t - image
+        z_ref[x + 2] = e_ref[x + 2] * t - image
         x_ref[x] = t
         return carry
 
-    lax.fori_loop(0, NX, residual, 0)
+    slabs_loop(residual, 0)
     first.sent()
 
     own_beam.wait()
@@ -517,7 +529,7 @@
     def zero_row():
         return jnp.zeros((8, NY), jnp.float32)
 
-    def all_sum(step, moments):
+    def all_sum(step, moments, meanwhile):
         lane = lax.broadcasted_iota(jnp.int32, (1, NY), 1)
         row = jnp.zeros((1, NY), jnp.float32)
         for n, m in enumerate(moments):
@@ -537,6 +549,7 @@
                     device_id_type=MESH,
                 ).start()
             slots[step, me] = row
+            meanwhile[phase]()
             most = slots.at[step, pl.ds(0, len(ring))]
             pltpu.make_async_copy(most, most, red_recv.at[step, phase]).wait()
             parts = [slots[step, n] for n in range(len(ring) + 1)]
@@ -551,59 +564,96 @@
     def folded(v):
         return v[0:8] + v[8:16] + v[16:24]
 
+    frame_bytes(0, beam_recv).wait()
+
+    def add_flux(x, pack):
+        tile = flux_tile(0, x)
+        fd_ref[0, x + 2] = tile
+        z_ref[x + 2, NZ - 8 : NZ, :] = z_ref[x + 2, NZ - 8 : NZ, :] + tile
+        return packed_into(pack, z_ref[x + 2], x)
+
+    z_pack = slabs_loop(add_flux, zero)
+    z_swap.pack[0] = z_pack
+    z_swap.start(z_ref.at[pl.ds(2, 2)], z_ref.at[pl.ds(NX, 2)])
+    e_swap.start(e_ref.at[pl.ds(2, 2)], e_ref.at[pl.ds(NX, 2)])
+    z_swap.arrive()
+    for at, slab in zip(GHOSTS, z_swap.slabs(0)):
+        z_ref[at] = slab
+    z_halo, z_corner = z_swap.halo(0), z_swap.corner(0)
+
+    def later_fluxes():
+        frame_bytes(1, beam_recv).wait()
+        frame_bytes(2, beam_recv).wait()
+
+        def next_flux(x, packs):
+            second, third = flux_tile(1, x), flux_tile(2, x)
+            third = third - second
+            second = second - fd_ref[0, x + 2]
+            fd_ref[1, x + 2] = second
+            fd_ref[2, x + 2] = third
+            return packed_into(packs[0], second, x), packed_into(packs[1], third, x)
+
+        packs = slabs_loop(next_flux, (zero_row(),) * 2)
+        f_swap.pack[0], f_swap.pack[1] = packs
+        f_swap.start(fd_ref.at[pl.ds(1, 2), pl.ds(2, 2)], fd_ref.at[pl.ds(1, 2), pl.ds(NX, 2)])
+
     for step in range(STEPS):
-        exchange = exchanges[1 + step]
-        if step == 0:
-            frame_bytes(0, beam_recv).wait()
-
-            def add_flux(x, pack):
-                tile = flux_tile(0, x)
-                fd_ref[0, x] = tile
-                z_ref[x + 2, NZ - 8 : NZ, :] = z_ref[x + 2, NZ - 8 : NZ, :] + tile
-                return packed_into(pack, z_ref[x + 2], x)
-
-            z_pack = lax.fori_loop(0, NX, add_flux, zero)
-        exchange.pack[0] = z_pack
-        exchange.start(z_ref.at[pl.ds(2, 2)], z_ref.at[pl.ds(NX, 2)])
-        if step + 1 < STEPS:
-            frame_bytes(step + 1, beam_recv).wait()
-
-            def next_flux(x, carry):
-                fd_ref[step + 1, x] = flux_tile(step + 1, x)
-                return carry
-
-            lax.fori_loop(0, NX, next_flux, 0)
-        exchange.arrive()
-        slabs = exchange.slabs(0)
-        for at, slab in zip((0, 1, NX + 2, NX + 3), slabs):
-            z_ref[at] = slab
-        z_halo, z_corner = exchange.halo(0), exchange.corner(0)
-
         u_ref[1] = apply_slab(z_ref, 1, side_tile(z_corner, 0), g_ref, 0)
         u_ref[NX + 2] = apply_slab(z_ref, NX + 2, side_tile(z_corner, NX - 1), g_ref, NX + 1)
         u_halo = apply_halo(z_halo, z_corner, z_pack, gp_ref)
-
-        def first_image(x, sums):
+        swap = uv_swaps[step] if step + 1 < STEPS else None
+
+        def first_image(x, carry):
+            sums, pack = carry
             u = apply_slab(z_ref, x + 2, side_tile(z_halo, x), g_ref, x + 1)
             u_ref[x + 2] = u
             z = z_ref[x + 2]
             dz = d_ref[x] * z
             du = d_ref[x] * u
-            return (
+            sums = (
                 sums[0] + folded(dz * z),
                 sums[1] + folded(dz * u),
                 sums[2] + folded(du * u),
             )
-
-        sums = lax.fori_loop(0, NX, first_image, (zero_row(),) * 3)
-
-        def second_image(x, acc):
+            return sums, (packed_into(pack, u, x) if swap else pack)
+
+        sums, u_pack = slabs_loop(first_image, ((zero_row(),) * 3, zero))
+
+        def second_image(x, carry):
+            acc, pack = carry
             v = apply_slab(u_ref, x + 2, side_tile(u_halo, x), g_ref, x + 1)
-            v_ref[x] = v
-            return acc + folded(d_ref[x] * u_ref[x + 2] * v)
-
-        last = lax.fori_loop(0, NX, second_image, zero_row())
-        g0, a, w, t, *rest = all_sum(step, list(sums) + [last] + ([bad] if step == 0 else []))
+            v_ref[x + 2] = v
+            acc = acc + folded(d_ref[x] * u_ref[x + 2] * v)
+            return acc, (packed_into(pack, v, x) if swap else pack)
+
+        last, v_pack = slabs_loop(second_image, (zero_row(), zero))
+
+        def send_images():
+            if swap:
+                swap.pack[0] = u_pack
+                swap.pack[1] = v_pack
+                swap.start(uv_ref.at[:, pl.ds(2, 2)], uv_ref.at[:, pl.ds(NX, 2)])
+            if step == 0:
+                later_fluxes()
+
+        def receive_images():
+            if step == 0:
+                z_swap.sent()
+                e_swap.arrive()
+                for at, slab in zip(GHOSTS, e_swap.slabs(0)):
+                    e_ref[at] = slab
+                f_swap.arrive()
+                for n in range(2):
+                    for at, slab in zip(GHOSTS, f_swap.slabs(n)):
+                        fd_ref[1 + n, at] = slab
+            if swap:
+                swap.arrive()
+
+        g0, a, w, t, *rest = all_sum(
+            step,
+            list(sums) + [last] + ([bad] if step == 0 else []),
+            (send_images, receive_images),
+        )
         if step == 0:
             flag_out[...] = jnp.broadcast_to(rest[0], (8, NY))
         alpha0 = g0 / a
@@ -612,30 +662,40 @@
         alpha1 = gamma1 / (beta1 * beta1 * a - 2.0 * beta1 * alpha0 * w + alpha0 * alpha0 * t)
         d1 = jnp.broadcast_to(alpha0 + alpha1 * beta1, (NZ, NY))
         d2 = jnp.broadcast_to(-alpha0 * alpha1, (NZ, NY))
-        exchange.sent()
-
-        if step + 1 < STEPS:
+
+        def next_z(z, u, v, e, tile):
+            z = z - d1 * u - d2 * v + e * (d1 * z + d2 * u)
+            return jnp.concatenate([z[: NZ - 8], z[NZ - 8 :] + tile], axis=0)
+
+        if swap:
+            for at, u, v in zip(GHOSTS, swap.slabs(0), swap.slabs(1)):
+                z_ref[at] = next_z(z_ref[at], u, v, e_ref[at], fd_ref[step + 1, at])
+            z_halo, z_corner = (
+                next_z(z, get(swap, 0), get(swap, 1), get(e_swap, 0), get(f_swap, step))
+                for z, get in ((z_halo, Exchange.halo), (z_corner, Exchange.corner))
+            )
 
             def update(x, pack):
-                z, u, v = z_ref[x + 2], u_ref[x + 2], v_ref[x]
-                move = d1 * z + d2 * u
-                x_ref[x] = x_ref[x] + move
-                z_ref[x + 2] = z - d1 * u - d2 * v + e_ref[x] * move
-                tile = fd_ref[step + 1, x] - fd_ref[step, x]
-                z_ref[x + 2, NZ - 8 : NZ, :] = z_ref[x + 2, NZ - 8 : NZ, :] + tile
-                return packed_into(pack, z_ref[x + 2], x)
-
-            z_pack = lax.fori_loop(0, NX, update, zero)
+                z, u, v = z_ref[x + 2], u_ref[x + 2], v_ref[x + 2]
+                x_ref[x] = x_ref[x] + (d1 * z + d2 * u)
+                z = next_z(z, u, v, e_ref[x + 2], fd_ref[step + 1, x + 2])
+                z_ref[x + 2] = z
+                return packed_into(pack, z, x)
+
+            z_pack = slabs_loop(update, zero)
+            swap.sent()
         else:
 
             def finish(x, carry):
-                z, u, v = z_ref[x + 2], u_ref[x + 2], v_ref[x]
+                z, u, v = z_ref[x + 2], u_ref[x + 2], v_ref[x + 2]
                 x_out[pl.ds(x, NZ, stride=NX), :] = x_ref[x] + (d1 * z + d2 * u)
                 r_out[pl.ds(x, NZ, stride=NX), :] = d_ref[x] * (z - d1 * u - d2 * v)
                 return carry
 
-            lax.fori_loop(0, NX, finish, 0)
-
+            slabs_loop(finish, 0)
+
+    e_swap.sent()
+    f_swap.sent()
     for frame in range(STEPS):
         frame_bytes(frame, beam_send).wait()
     for step in range(STEPS):
@@ -644,7 +704,7 @@
             pltpu.make_async_copy(most, most, red_send.at[step, phase]).wait()
 
 
-def exchange_scratch(fields, rows=NZ):
+def exchange_scratch(fields, rows):
     f32 = jnp.float32
     return [
         pltpu.VMEM((2, fields, 2, rows, NY), f32),
@@ -678,14 +738,13 @@
         pltpu.VMEM((6, NX, 8, NY), f32),
         pltpu.VMEM((3, NX + 4, NZ, NY), f32),
         pltpu.VMEM((NX + 4, NZ, NY), f32),
-        pltpu.VMEM((NX + 4, NZ, NY), f32),
-        pltpu.VMEM((NX, NZ, NY), f32),
+        pltpu.VMEM((2, NX + 4, NZ, NY), f32),
         pltpu.VMEM((NX, NZ, NY), f32),
         pltpu.VMEM((6, NX + 2, NZ, NY), f32),
         pltpu.VMEM((6, NZ, NY), f32),
         pltpu.VMEM((NX, NZ, NY), f32),
-        pltpu.VMEM((NX, NZ, NY), f32),
-        pltpu.VMEM((STEPS, NX, 8, NY), f32),
+        pltpu.VMEM((NX + 4, NZ, NY), f32),
+        pltpu.VMEM((STEPS, NX + 4, 8, NY), f32),
         pltpu.VMEM((STEPS, 2, 1, NY), f32),
         pltpu.VMEM((STEPS, NPX, 1, NY), f32),
         pltpu.VMEM((STEPS, NPY, 1, NY), f32),
@@ -695,8 +754,8 @@
         pltpu.SemaphoreType.DMA((STEPS, 2)),
         pltpu.SemaphoreType.DMA((STEPS, 2)),
     ]
-    for fields in (3, 1, 1, 1):
-        scratch += exchange_scratch(fields)
+    for fields, rows in EXCHANGES:
+        scratch += exchange_scratch(fields, rows)
     warmth, leftover, flag = pl.pallas_call(
         kernel,
         out_shape=(

time: 96.6 us -> 62.9 us (0.65)
  Pallas kernels: 90.7 us -> 57 us
    pallas_call x1, Pallas kernels: 90.7 us -> 57 us  [body(): pl.pallas_call(kernel, out_shape=(jax.ShapeDtypeStruct(flat, f32), jax.Sh...]
where the time goes in v2:
time: 62.9 us; the launch traced here: 62.7 us
  Pallas kernels  57 us (91%)
  local copies, waits for them, and re-layouts  4.07 us (6%)
  between operations  1.4 us (2%)
    pallas_call x1, Pallas kernels, body(): pl.pallas_call(kernel, out_shape=(jax.ShapeDtypeStruct(flat, f32), jax.Sh...  57 us
    unnamed x14, local copies, waits for them, and re-layouts  3.56 us

profile of v2, /device:TPU:0, one launch (start us, length us, event | category | flops | bytes accessed | tf_op | source)
XLA Modules:
  0.0 62.7 jit_solution(6592248602535976974)
XLA Ops:
  0.6 0.0 copy-start.10
  0.6 0.0 copy-start.18
  0.7 0.0 copy-start.19
  0.7 0.0 copy-start.1
  0.7 0.0 copy-start
  0.7 0.0 copy-start.3
  0.7 57.0 %shard_map.81 = (f32[768,128]{1,0:T(8,128)}, f32[768,128]{1,0:T(8,128)}, f32[8,128]{1,0:T(8,128)S(1)}) custom-call(f32[3,16,2048]{2,1,0:T(8,128)} %beam.1, s32[8,32,128]{2,1,0:T(8,128)} %loc_in.1, f32[8,32,128]{2,1,0:T(8,128)} %share_in.1, f32[768,128]{1,0:T(8,128)} %bitcast.38, f32[768,128]{1,0:T(8,128)} %bitcast.37, f32[768,128]{1,0:T(8,128)} %bitcast.39), custom_call_target="tpu_custom_call" | custom-call | tf_op jit(solution)/shard_map/pallas_call | solution.py:759
  57.7 0.5 slice.478
  58.8 0.0 copy-done.10
  58.9 0.0 copy-done.18
  58.9 0.0 copy-done.19
  58.9 0.0 copy-done.1
  58.9 0.0 copy-done
  58.9 0.0 copy-done.3
  58.9 0.2 conditional.1
  59.1 1.8 %copy.39 = f32[24,32,128]{2,1,0:T(8,128)} copy(f32[24,32,128]{2,1,0:T(8,128)} %get-tuple-element.177) | data formatting | bytes 786432
  60.9 1.8 %copy.40 = f32[24,32,128]{2,1,0:T(8,128)} copy(f32[24,32,128]{2,1,0:T(8,128)} %get-tuple-element.178) | data formatting | bytes 786432
Async XLA Ops:
  0.6 58.2 %copy-start.10 = (f32[3,16,2048]{2,1,0:T(8,128)S(1)}, f32[3,16,2048]{2,1,0:T(8,128)}, u32[]{:S(2)}) copy-start(f32[3,16,2048]{2,1,0:T(8,128)} %beam.1) | copy-start | bytes 1179652
  0.6 58.2 %copy-start.18 = (s32[8,32,128]{2,1,0:T(8,128)S(1)}, s32[8,32,128]{2,1,0:T(8,128)}, u32[]{:S(2)}) copy-start(s32[8,32,128]{2,1,0:T(8,128)} %loc_in.1) | copy-start | bytes 393220
  0.7 58.2 %copy-start.19 = (f32[8,32,128]{2,1,0:T(8,128)S(1)}, f32[8,32,128]{2,1,0:T(8,128)}, u32[]{:S(2)}) copy-start(f32[8,32,128]{2,1,0:T(8,128)} %share_in.1) | copy-start | bytes 393220
  0.7 58.2 %copy-start.1 = (f32[24,32,128]{2,1,0:T(8,128)S(1)}, f32[24,32,128]{2,1,0:T(8,128)}, u32[]{:S(2)}) copy-start(f32[24,32,128]{2,1,0:T(8,128)} %param.17) | copy-start | bytes 1179652
  0.7 58.2 %copy-start = (f32[24,32,128]{2,1,0:T(8,128)S(1)}, f32[24,32,128]{2,1,0:T(8,128)}, u32[]{:S(2)}) copy-start(f32[24,32,128]{2,1,0:T(8,128)} %param.18) | copy-start | bytes 1179652
  0.7 58.2 %copy-start.3 = (f32[24,32,128]{2,1,0:T(8,128)S(1)}, f32[24,32,128]{2,1,0:T(8,128)}, u32[]{:S(2)}) copy-start(f32[24,32,128]{2,1,0:T(8,128)} %param.19) | copy-start | bytes 1179652

commit v3 on v2

--- a/solution.py
+++ b/solution.py
@@ -420,8 +420,8 @@
         most = window.at[frame, pl.ds(0, (NPY - 1) * BR), :]
         return pltpu.make_async_copy(most, most, sem.at[frame])
 
+    first.start(kct.at[:, 2:4], kct.at[:, NX : NX + 2])
     send_frame(0)
-    first.start(kct.at[:, 2:4], kct.at[:, NX : NX + 2])
     for frame in range(1, STEPS):
         send_frame(frame)
 
@@ -655,7 +655,7 @@
             (send_images, receive_images),
         )
         if step == 0:
-            flag_out[...] = jnp.broadcast_to(rest[0], (8, NY))
+            flag_out[0] = jnp.where(jnp.sum(rest[0]) > 0.0, 1, 0).astype(jnp.int32)
         alpha0 = g0 / a
         gamma1 = alpha0 * alpha0 * w - g0
         beta1 = 1.0 + gamma1 / g0
@@ -714,6 +714,28 @@
         pltpu.SemaphoreType.DMA((8,)),
         pltpu.SemaphoreType.DMA((8,)),
     ]
+
+
+def hand_on(a_in, b_in, a_out, b_out, sem):
+    copies = [
+        pltpu.make_async_copy(src, dst, sem.at[n])
+        for n, (src, dst) in enumerate(((a_in, a_out), (b_in, b_out)))
+    ]
+    for copy in copies:
+        copy.start()
+    for copy in copies:
+        copy.wait()
+
+
+def handed_on(a, b):
+    space = pl.BlockSpec(memory_space=pl.ANY)
+    return pl.pallas_call(
+        hand_on,
+        out_shape=(jax.ShapeDtypeStruct(a.shape, a.dtype), jax.ShapeDtypeStruct(b.shape, b.dtype)),
+        in_specs=[space, space],
+        out_specs=(space, space),
+        scratch_shapes=[pltpu.SemaphoreType.DMA((2,))],
+    )(a, b)
 
 
 def body(
@@ -761,10 +783,10 @@
         out_shape=(
             jax.ShapeDtypeStruct(flat, f32),
             jax.ShapeDtypeStruct(flat, f32),
-            jax.ShapeDtypeStruct((8, NY), f32),
+            jax.ShapeDtypeStruct((1,), jnp.int32),
         ),
         in_specs=[hbm] * 6,
-        out_specs=(vmem, vmem, vmem),
+        out_specs=(vmem, vmem, pl.BlockSpec(memory_space=pltpu.SMEM)),
         scratch_shapes=scratch,
         compiler_params=pltpu.CompilerParams(
             collective_id=0, has_side_effects=True, vmem_limit_bytes=40 * 2**20
@@ -778,18 +800,21 @@
         thermal_storage.reshape(flat),
     )
     shape = starting_warmth.shape
-    return lax.cond(
-        flag[0, 0] > 0.0,
-        lambda: general(
-            incident_power_density,
-            coupling_patch_locator,
-            coupling_share_factor,
-            starting_warmth,
-            diffusive_coefficient,
-            thermal_storage,
+    out = lax.cond(
+        flag[0] > 0,
+        lambda: list(
+            general(
+                incident_power_density,
+                coupling_patch_locator,
+                coupling_share_factor,
+                starting_warmth,
+                diffusive_coefficient,
+                thermal_storage,
+            )
         ),
-        lambda: (warmth.reshape(shape), leftover.reshape(shape)),
+        lambda: [out.reshape(shape) for out in handed_on(warmth, leftover)],
     )
+    return tuple(out)
 
 
 def solution(mesh):

time: 62.9 us -> 58.6 us (0.932)
  local copies, waits for them, and re-layouts: 4.07 us -> 0.03 us
    unnamed x14 -> x12, local copies, waits for them, and re-layouts: 3.56 us -> 0.03 us
    pallas_call x1, Pallas kernels: 57 us -> 55.8 us  [body(): pl.pallas_call(kernel, out_shape=(jax.ShapeDtypeStruct(flat, f32), jax.Sh...]
    pallas_call x0 -> x1, Pallas kernels: none -> 0.89 us  [handed_on(): pl.pallas_call(hand_on, out_shape=(jax.ShapeDtypeStruct(a.shape, a.dtype)...]
where the time goes in v3:
time: 58.6 us; the launch traced here: 58.4 us
  Pallas kernels  56.7 us (97%)
  between operations  1.47 us (3%)
    pallas_call x1, Pallas kernels, body(): pl.pallas_call(kernel, out_shape=(jax.ShapeDtypeStruct(flat, f32), jax.Sh...  55.8 us

profile of v3, /device:TPU:0, one launch (start us, length us, event | category | flops | bytes accessed | tf_op | source)
XLA Modules:
  0.0 58.4 jit_solution(2658271440779838085)
XLA Ops:
  0.6 0.0 copy-start.10
  0.6 0.0 copy-start.18
  0.7 0.0 copy-start.19
  0.7 0.0 copy-start.1
  0.7 0.0 copy-start
  0.7 0.0 copy-start.3
  0.7 55.8 %shard_map.81 = (f32[768,128]{1,0:T(8,128)S(1)}, f32[768,128]{1,0:T(8,128)S(1)}, s32[1]{0:T(128)}) custom-call(f32[3,16,2048]{2,1,0:T(8,128)} %beam.1, s32[8,32,128]{2,1,0:T(8,128)} %loc_in.1, f32[8,32,128]{2,1,0:T(8,128)} %share_in.1, f32[768,128]{1,0:T(8,128)} %bitcast.38, f32[768,128]{1,0:T(8,128)} %bitcast.37, f32[768,128]{1,0:T(8,128)} %bitcast.39), custom_call_target="tpu_custom_call" | custom-call | tf_op jit(solution)/shard_map/pallas_call | solution.py:781
  57.1 0.0 copy-done.10
  57.1 0.0 copy-done.18
  57.1 0.0 copy-done.19
  57.1 0.0 copy-done.1
  57.1 0.0 copy-done
  57.1 0.0 copy-done.3
  57.1 1.1 %conditional.1 = (f32[24,32,128]{2,1,0:T(8,128)}, f32[24,32,128]{2,1,0:T(8,128)}) conditional(s32[]{:T(128)} %bitcast.24, (f32[768,128]{1,0:T(8,128)S(1)}, f32[768,128]{1,0:T(8,128)S(1)}) %tuple.27, (f32[24,32,128]{2,1,0:T(8,128)S(1)}, f32[24,32,128]{2,1,0:T(8,128)S(1)}, f32[3,16,2048]{2,1,0:T(8,128)S(1)}, s32[8,32,128]{2,1,0:T(8,128)S(1)}, ...), branch_computations={%region_0.0_spmd, %region_1.29_spmd} | conditional | flops 49728704 | bytes 95354696 | solution.py:803
  57.1 0.9 %branch_0_fun.1 = (f32[768,128]{1,0:T(8,128)}, f32[768,128]{1,0:T(8,128)}) custom-call(f32[768,128]{1,0:T(8,128)S(1)} %get-tuple-element.52.a_in, f32[768,128]{1,0:T(8,128)S(1)} %get-tuple-element.53.b_in), custom_call_target="tpu_custom_call" | custom-call | tf_op jit(solution)/shard_map/cond/branch_0_fun/pallas_call | solution.py:732
Async XLA Ops:
  0.6 56.4 %copy-start.10 = (f32[3,16,2048]{2,1,0:T(8,128)S(1)}, f32[3,16,2048]{2,1,0:T(8,128)}, u32[]{:S(2)}) copy-start(f32[3,16,2048]{2,1,0:T(8,128)} %beam.1) | copy-start | bytes 1179652
  0.6 56.4 %copy-start.18 = (s32[8,32,128]{2,1,0:T(8,128)S(1)}, s32[8,32,128]{2,1,0:T(8,128)}, u32[]{:S(2)}) copy-start(s32[8,32,128]{2,1,0:T(8,128)} %loc_in.1) | copy-start | bytes 393220
  0.7 56.4 %copy-start.19 = (f32[8,32,128]{2,1,0:T(8,128)S(1)}, f32[8,32,128]{2,1,0:T(8,128)}, u32[]{:S(2)}) copy-start(f32[8,32,128]{2,1,0:T(8,128)} %share_in.1) | copy-start | bytes 393220
  0.7 56.4 %copy-start.1 = (f32[24,32,128]{2,1,0:T(8,128)S(1)}, f32[24,32,128]{2,1,0:T(8,128)}, u32[]{:S(2)}) copy-start(f32[24,32,128]{2,1,0:T(8,128)} %param.17) | copy-start | bytes 1179652
  0.7 56.4 %copy-start = (f32[24,32,128]{2,1,0:T(8,128)S(1)}, f32[24,32,128]{2,1,0:T(8,128)}, u32[]{:S(2)}) copy-start(f32[24,32,128]{2,1,0:T(8,128)} %param.18) | copy-start | bytes 1179652
  0.7 56.4 %copy-start.3 = (f32[24,32,128]{2,1,0:T(8,128)S(1)}, f32[24,32,128]{2,1,0:T(8,128)}, u32[]{:S(2)}) copy-start(f32[24,32,128]{2,1,0:T(8,128)} %param.19) | copy-start | bytes 1179652

commit v4 on v3

--- a/solution.py
+++ b/solution.py
@@ -188,7 +188,7 @@
 
 
 GHOSTS = (0, 1, NX + 2, NX + 3)
-EXCHANGES = ((3, NZ), (1, NZ), (1, NZ), (2, 8), (2, NZ), (2, NZ))
+EXCHANGES = ((1, NZ), (1, NZ), (2, 8))
 CORNERS = ((-1, 1), (-1, -1), (1, 1), (1, -1))
 
 
@@ -196,36 +196,42 @@
     def __init__(self, place, refs):
         self.place = place
         self.rx, self.rs, self.rk, self.pack, self.send, self.recv = refs
-        self.copies = []
-
-    def start(self, low, high):
-        place = self.place
+
+    def plan(self, low, high):
+        to_right, to_left = self.packs()
         plan = []
         for n, (dx, dy) in enumerate(CORNERS):
-            plan.append((self.pack, self.rk.at[n], (-dx, -dy)))
-        plan.append((self.pack, self.rs.at[0], (0, 1)))
-        plan.append((self.pack, self.rs.at[1], (0, -1)))
-        single = len(low.shape) == 3
+            plan.append((to_left if dy > 0 else to_right, self.rk.at[n], (-dx, -dy)))
+        plan.append((to_right, self.rs.at[0], (0, 1)))
+        plan.append((to_left, self.rs.at[1], (0, -1)))
+        single = len(low.shape) + 2 == len(self.rx.shape)
         for n, (src, dx) in enumerate(((high, 1), (low, -1))):
             plan.append((src, self.rx.at[n, 0] if single else self.rx.at[n], (dx, 0)))
-        for n, (src, dst, (dx, dy)) in enumerate(plan):
-            copy = pltpu.make_async_remote_copy(
+        return [
+            pltpu.make_async_remote_copy(
                 src_ref=src,
                 dst_ref=dst,
                 send_sem=self.send.at[n],
                 recv_sem=self.recv.at[n],
-                device_id=place.at(dx, dy),
+                device_id=self.place.at(dx, dy),
                 device_id_type=MESH,
             )
+            for n, (src, dst, (dx, dy)) in enumerate(plan)
+        ]
+
+    def packs(self):
+        return self.pack, self.pack
+
+    def start(self, *edges):
+        for copy in self.plan(*edges):
             copy.start()
-            self.copies.append(copy)
-
-    def arrive(self):
-        for copy in self.copies:
+
+    def arrive(self, *edges):
+        for copy in self.plan(*edges):
             copy.wait_recv()
 
-    def sent(self):
-        for copy in self.copies:
+    def sent(self, *edges):
+        for copy in self.plan(*edges):
             copy.wait_send()
 
     def slabs(self, field):
@@ -237,26 +243,63 @@
             self.rx[1, field, 1] * p.has_high,
         )
 
+    def sides(self, field):
+        return self.rs[0, field], self.rs[1, field], (-3, -1, 1, 3)
+
+    def corners(self, field):
+        return [self.rk[n, field] for n in range(4)], (3, 5, -5, -3)
+
     def halo(self, field):
         p = self.place
-        left = self.rs[0, field] * p.has_left
-        right = self.rs[1, field] * p.has_right
+        left, right, shifts = self.sides(field)
+        left, right = left * p.has_left, right * p.has_right
         j = lax.rem(lanes(left.shape[0]), 4)
-        far = jnp.where(j == 0, rolled(right, -3), rolled(left, 3))
-        near = jnp.where(j == 1, rolled(right, -1), rolled(left, 1))
+        far = jnp.where(j == 0, rolled(right, shifts[0]), rolled(left, shifts[3]))
+        near = jnp.where(j == 1, rolled(right, shifts[1]), rolled(left, shifts[2]))
         return jnp.where((j == 1) | (j == 2), near, far)
 
     def corner(self, field):
         p = self.place
-        a = rolled(self.rk[0, field] * (p.has_low * p.has_right), 3)
-        b = rolled(self.rk[1, field] * (p.has_low * p.has_left), 5)
-        c = rolled(self.rk[2, field] * (p.has_high * p.has_right), -5)
-        d = rolled(self.rk[3, field] * (p.has_high * p.has_left), -3)
-        lane = lanes(a.shape[0])
-        out = jnp.where(lane == 1, a, jnp.zeros_like(a))
-        out = jnp.where(lane == 2, b, out)
-        out = jnp.where(lane == NY - 3, c, out)
-        return jnp.where(lane == NY - 2, d, out)
+        tiles, shifts = self.corners(field)
+        masks = (
+            p.has_low * p.has_right,
+            p.has_low * p.has_left,
+            p.has_high * p.has_right,
+            p.has_high * p.has_left,
+        )
+        lane = lanes(tiles[0].shape[0])
+        out = jnp.zeros_like(tiles[0])
+        for at, tile, mask, shift in zip((1, 2, NY - 3, NY - 2), tiles, masks, shifts):
+            out = jnp.where(lane == at, rolled(tile * mask, shift), out)
+        return out
+
+
+class PairExchange(Exchange):
+    def packs(self):
+        return self.pack.at[0], self.pack.at[1]
+
+    def fill(self, first, second):
+        j = lax.rem(lanes(), 4)
+        self.pack[0] = jnp.where(j < 2, first, rolled(second, 2))
+        self.pack[1] = jnp.where(j < 2, rolled(first, -2), second)
+
+    def sides(self, field):
+        return self.rs[0], self.rs[1], ((-3, -1, -1, 1) if field else (-1, 1, 1, 3))
+
+    def corners(self, field):
+        return [self.rk[n] for n in range(4)], ((3, 3, -5, -5) if field else (5, 5, -3, -3))
+
+
+class FirstExchange(PairExchange):
+    def fill(self, k, c, t):
+        j = lax.rem(lanes(), 4)
+        right = jnp.where(j == 2, rolled(c, 1), rolled(t, 2))
+        left = jnp.where(j == 2, c, rolled(t, 1))
+        self.pack[0] = jnp.where(j < 2, k, right)
+        self.pack[1] = jnp.where(j < 2, rolled(k, -2), left)
+
+    def sides(self, field):
+        return self.rs[0], self.rs[1], ((-1, 1, 1, 3), (0, -1, 0, 0), (0, -2, -1, 0))[field]
 
 
 def packed_into(pack, v, x):
@@ -308,6 +351,10 @@
     d_ref,
     e_ref,
     fd_ref,
+    z_near,
+    e_near,
+    f_near,
+    uv_near,
     red_src,
     red_px,
     red_py,
@@ -352,11 +399,22 @@
     exchanges = [
         Exchange(place, exchange_refs[6 * n : 6 * n + 6]) for n in range(len(EXCHANGES))
     ]
-    first, z_swap, e_swap, f_swap, *uv_swaps = exchanges
+    z_swap, e_swap, f_swap = exchanges
+    first = FirstExchange(place, exchange_refs[-13:-7])
+    k_edge = exchange_refs[-7]
+    uv_refs = exchange_refs[-6:]
+    k_edges = k_edge.at[0], k_edge.at[1]
+    z_edges = z_ref.at[pl.ds(2, 2)], z_ref.at[pl.ds(NX, 2)]
+    e_edges = e_ref.at[pl.ds(2, 2)], e_ref.at[pl.ds(NX, 2)]
+    f_edges = fd_ref.at[pl.ds(1, 2), pl.ds(2, 2)], fd_ref.at[pl.ds(1, 2), pl.ds(NX, 2)]
+    uv_edges = uv_ref.at[:, pl.ds(2, 2)], uv_ref.at[:, pl.ds(NX, 2)]
 
     for copy in local[:3]:
         copy.wait()
     zero = jnp.zeros((NZ, NY), jnp.float32)
+
+    def zero_row():
+        return jnp.zeros((8, NY), jnp.float32)
 
     def lay(x, packs):
         out = []
@@ -368,8 +426,11 @@
 
     packs = slabs_loop(lay, (zero, zero, zero))
     k_pack, c_pack, t_pack = packs
-    for n in range(3):
-        first.pack[n] = packs[n]
+    first.fill(*packs)
+    edges = ((0, 0, NX - 2), (0, 1, NX - 1), (1, 0, NX - 1), (2, 0, NX - 1))
+    for n, (field, low, high) in enumerate(edges):
+        k_edge[0, n] = kct[field, low + 2]
+        k_edge[1, n] = kct[field, high + 2]
 
     local[3].wait()
     local[4].wait()
@@ -403,8 +464,12 @@
     pl.semaphore_wait(barrier, len(everyone))
 
     def send_frame(frame):
-        copies = []
-        for device in py_ring:
+        def send_block(n, nothing):
+            n = jnp.where(n < 10, n, n + 1)
+            device = (
+                place.px,
+                lax.rem(place.py // 4 + 2 + n // 4, 4) * 4 + lax.rem(lax.rem(place.py, 4) + 2 + lax.rem(n, 4), 4),
+            )
             columns = pl.ds(pl.multiple_of(device[1] * NY, NY), NY)
             copy = pltpu.make_async_remote_copy(
                 src_ref=beam.at[frame, :, columns],
@@ -415,23 +480,26 @@
                 device_id_type=MESH,
             )
             copy.start()
+            return nothing
+
+        lax.fori_loop(0, NPY - 1, send_block, 0)
 
     def frame_bytes(frame, sem):
         most = window.at[frame, pl.ds(0, (NPY - 1) * BR), :]
         return pltpu.make_async_copy(most, most, sem.at[frame])
 
-    first.start(kct.at[:, 2:4], kct.at[:, NX : NX + 2])
+    first.start(*k_edges)
     send_frame(0)
     for frame in range(1, STEPS):
         send_frame(frame)
 
-    first.arrive()
-    for n in range(3):
-        slabs = first.slabs(n)
-        for at, slab in zip(GHOSTS, slabs):
-            kct[n, at] = slab
+    first.arrive(*k_edges)
+    for n, (field, low, high) in enumerate(edges):
+        kct[field, high + 2 - NX] = first.rx[0, n] * place.has_low
+        kct[field, low + 2 + NX] = first.rx[1, n] * place.has_high
     k_halo, k_corner = first.halo(0), first.corner(0)
     c_halo, t_halo = first.halo(1), first.halo(2)
+    c_halo = jnp.where((lax.rem(lanes(), 4) + 1) // 2 == 1, c_halo, 0.0)
     level = lax.broadcasted_iota(jnp.int32, (NZ, NY), 0)
 
     def over(k, up, down, below, above, left, right, storage, mask):
@@ -502,12 +570,13 @@
     def residual(x, carry):
         image = apply_slab(t_ref, x + 2, side_tile(t_halo, x), g_ref, x + 1)
         t = t_ref[x + 2]
-        z_ref[x + 2] = e_ref[x + 2] * t - image
+        z = e_ref[x + 2] * t - image
+        z_ref[x + 2] = z
         x_ref[x] = t
-        return carry
-
-    slabs_loop(residual, 0)
-    first.sent()
+        return packed_into(carry, z, x)
+
+    z_near[2] = slabs_loop(residual, zero)
+    first.sent(*k_edges)
 
     own_beam.wait()
 
@@ -525,9 +594,6 @@
         flux = jnp.sum(part, axis=0, keepdims=True)
         top = d_ref[x, NZ - 8 : NZ, :]
         return jnp.where(row8 == 7, flux, 0.0) / top
-
-    def zero_row():
-        return jnp.zeros((8, NY), jnp.float32)
 
     def all_sum(step, moments, meanwhile):
         lane = lax.broadcasted_iota(jnp.int32, (1, NY), 1)
@@ -570,16 +636,16 @@
         tile = flux_tile(0, x)
         fd_ref[0, x + 2] = tile
         z_ref[x + 2, NZ - 8 : NZ, :] = z_ref[x + 2, NZ - 8 : NZ, :] + tile
-        return packed_into(pack, z_ref[x + 2], x)
-
-    z_pack = slabs_loop(add_flux, zero)
-    z_swap.pack[0] = z_pack
-    z_swap.start(z_ref.at[pl.ds(2, 2)], z_ref.at[pl.ds(NX, 2)])
-    e_swap.start(e_ref.at[pl.ds(2, 2)], e_ref.at[pl.ds(NX, 2)])
-    z_swap.arrive()
+        return packed_into(pack, tile, x)
+
+    z_near[2, NZ - 8 : NZ] = z_near[2, NZ - 8 : NZ] + slabs_loop(add_flux, zero_row())
+    z_swap.pack[0] = z_near[2]
+    z_swap.start(*z_edges)
+    e_swap.start(*e_edges)
+    z_swap.arrive(*z_edges)
     for at, slab in zip(GHOSTS, z_swap.slabs(0)):
         z_ref[at] = slab
-    z_halo, z_corner = z_swap.halo(0), z_swap.corner(0)
+    z_near[0], z_near[1] = z_swap.halo(0), z_swap.corner(0)
 
     def later_fluxes():
         frame_bytes(1, beam_recv).wait()
@@ -595,13 +661,15 @@
 
         packs = slabs_loop(next_flux, (zero_row(),) * 2)
         f_swap.pack[0], f_swap.pack[1] = packs
-        f_swap.start(fd_ref.at[pl.ds(1, 2), pl.ds(2, 2)], fd_ref.at[pl.ds(1, 2), pl.ds(NX, 2)])
-
-    for step in range(STEPS):
+        f_swap.start(*f_edges)
+
+    def one_step(step, nothing):
+        swap = PairExchange(place, [ref.at[step] for ref in uv_refs])
+        more = step + 1 < STEPS
+        z_halo, z_corner = z_near[0], z_near[1]
         u_ref[1] = apply_slab(z_ref, 1, side_tile(z_corner, 0), g_ref, 0)
         u_ref[NX + 2] = apply_slab(z_ref, NX + 2, side_tile(z_corner, NX - 1), g_ref, NX + 1)
-        u_halo = apply_halo(z_halo, z_corner, z_pack, gp_ref)
-        swap = uv_swaps[step] if step + 1 < STEPS else None
+        u_halo = apply_halo(z_halo, z_corner, z_near[2], gp_ref)
 
         def first_image(x, carry):
             sums, pack = carry
@@ -615,7 +683,7 @@
                 sums[1] + folded(dz * u),
                 sums[2] + folded(du * u),
             )
-            return sums, (packed_into(pack, u, x) if swap else pack)
+            return sums, packed_into(pack, u, x)
 
         sums, u_pack = slabs_loop(first_image, ((zero_row(),) * 3, zero))
 
@@ -624,56 +692,59 @@
             v = apply_slab(u_ref, x + 2, side_tile(u_halo, x), g_ref, x + 1)
             v_ref[x + 2] = v
             acc = acc + folded(d_ref[x] * u_ref[x + 2] * v)
-            return acc, (packed_into(pack, v, x) if swap else pack)
+            return acc, packed_into(pack, v, x)
 
         last, v_pack = slabs_loop(second_image, (zero_row(), zero))
 
         def send_images():
-            if swap:
-                swap.pack[0] = u_pack
-                swap.pack[1] = v_pack
-                swap.start(uv_ref.at[:, pl.ds(2, 2)], uv_ref.at[:, pl.ds(NX, 2)])
-            if step == 0:
+            @pl.when(more)
+            def _():
+                swap.fill(u_pack, v_pack)
+                swap.start(*uv_edges)
+
+            @pl.when(step == 0)
+            def _():
                 later_fluxes()
 
         def receive_images():
-            if step == 0:
-                z_swap.sent()
-                e_swap.arrive()
+            @pl.when(step == 0)
+            def _():
+                z_swap.sent(*z_edges)
+                e_swap.arrive(*e_edges)
                 for at, slab in zip(GHOSTS, e_swap.slabs(0)):
                     e_ref[at] = slab
-                f_swap.arrive()
+                f_swap.arrive(*f_edges)
                 for n in range(2):
                     for at, slab in zip(GHOSTS, f_swap.slabs(n)):
                         fd_ref[1 + n, at] = slab
-            if swap:
-                swap.arrive()
-
-        g0, a, w, t, *rest = all_sum(
-            step,
-            list(sums) + [last] + ([bad] if step == 0 else []),
-            (send_images, receive_images),
+                e_near[0], e_near[1] = e_swap.halo(0), e_swap.corner(0)
+                for n in range(2):
+                    f_near[n, 0], f_near[n, 1] = f_swap.halo(n), f_swap.corner(n)
+
+            @pl.when(more)
+            def _():
+                swap.arrive(*uv_edges)
+                for n in range(2):
+                    uv_near[n, 0], uv_near[n, 1] = swap.halo(n), swap.corner(n)
+
+        g0, a, w, t, far = all_sum(
+            step, list(sums) + [last, bad], (send_images, receive_images)
         )
-        if step == 0:
-            flag_out[0] = jnp.where(jnp.sum(rest[0]) > 0.0, 1, 0).astype(jnp.int32)
-        alpha0 = g0 / a
-        gamma1 = alpha0 * alpha0 * w - g0
-        beta1 = 1.0 + gamma1 / g0
-        alpha1 = gamma1 / (beta1 * beta1 * a - 2.0 * beta1 * alpha0 * w + alpha0 * alpha0 * t)
-        d1 = jnp.broadcast_to(alpha0 + alpha1 * beta1, (NZ, NY))
-        d2 = jnp.broadcast_to(-alpha0 * alpha1, (NZ, NY))
+        flag_out[0] = jnp.where(jnp.sum(far) > 0.0, 1, 0).astype(jnp.int32)
+        inverse = 1.0 / (a * t - w * w)
+        d1 = jnp.broadcast_to((g0 * t - a * w) * inverse, (NZ, NY))
+        d2 = jnp.broadcast_to((a * a - g0 * w) * inverse, (NZ, NY))
 
         def next_z(z, u, v, e, tile):
             z = z - d1 * u - d2 * v + e * (d1 * z + d2 * u)
             return jnp.concatenate([z[: NZ - 8], z[NZ - 8 :] + tile], axis=0)
 
-        if swap:
+        @pl.when(more)
+        def _():
             for at, u, v in zip(GHOSTS, swap.slabs(0), swap.slabs(1)):
                 z_ref[at] = next_z(z_ref[at], u, v, e_ref[at], fd_ref[step + 1, at])
-            z_halo, z_corner = (
-                next_z(z, get(swap, 0), get(swap, 1), get(e_swap, 0), get(f_swap, step))
-                for z, get in ((z_halo, Exchange.halo), (z_corner, Exchange.corner))
-            )
+            for n in range(2):
+                z_near[n] = next_z(z_near[n], uv_near[0, n], uv_near[1, n], e_near[n], f_near[step, n])
 
             def update(x, pack):
                 z, u, v = z_ref[x + 2], u_ref[x + 2], v_ref[x + 2]
@@ -682,10 +753,11 @@
                 z_ref[x + 2] = z
                 return packed_into(pack, z, x)
 
-            z_pack = slabs_loop(update, zero)
-            swap.sent()
-        else:
-
+            z_near[2] = slabs_loop(update, zero)
+            swap.sent(*uv_edges)
+
+        @pl.when(not more)
+        def _():
             def finish(x, carry):
                 z, u, v = z_ref[x + 2], u_ref[x + 2], v_ref[x + 2]
                 x_out[pl.ds(x, NZ, stride=NX), :] = x_ref[x] + (d1 * z + d2 * u)
@@ -694,8 +766,12 @@
 
             slabs_loop(finish, 0)
 
-    e_swap.sent()
-    f_swap.sent()
+        return nothing
+
+    for step in range(STEPS):
+        one_step(step, 0)
+    e_swap.sent(*e_edges)
+    f_swap.sent(*f_edges)
     for frame in range(STEPS):
         frame_bytes(frame, beam_send).wait()
     for step in range(STEPS):
@@ -767,6 +843,10 @@
         pltpu.VMEM((NX, NZ, NY), f32),
         pltpu.VMEM((NX + 4, NZ, NY), f32),
         pltpu.VMEM((STEPS, NX + 4, 8, NY), f32),
+        pltpu.VMEM((3, NZ, NY), f32),
+        pltpu.VMEM((2, NZ, NY), f32),
+        pltpu.VMEM((2, 2, 8, NY), f32),
+        pltpu.VMEM((2, 2, NZ, NY), f32),
         pltpu.VMEM((STEPS, 2, 1, NY), f32),
         pltpu.VMEM((STEPS, NPX, 1, NY), f32),
         pltpu.VMEM((STEPS, NPY, 1, NY), f32),
@@ -778,6 +858,21 @@
     ]
     for fields, rows in EXCHANGES:
         scratch += exchange_scratch(fields, rows)
+    scratch += [
+        pltpu.VMEM((2, 4, NZ, NY), f32),
+        pltpu.VMEM((2, NZ, NY), f32),
+        pltpu.VMEM((4, NZ, NY), f32),
+        pltpu.VMEM((2, NZ, NY), f32),
+        pltpu.SemaphoreType.DMA((8,)),
+        pltpu.SemaphoreType.DMA((8,)),
+        pltpu.VMEM((2, 4, NZ, NY), f32),
+        pltpu.VMEM((STEPS - 1, 2, 2, 2, NZ, NY), f32),
+        pltpu.VMEM((STEPS - 1, 2, NZ, NY), f32),
+        pltpu.VMEM((STEPS - 1, 4, NZ, NY), f32),
+        pltpu.VMEM((STEPS - 1, 2, NZ, NY), f32),
+        pltpu.SemaphoreType.DMA((STEPS - 1, 8)),
+        pltpu.SemaphoreType.DMA((STEPS - 1, 8)),
+    ]
     warmth, leftover, flag = pl.pallas_call(
         kernel,
         out_shape=(

time: 58.6 us -> 56.8 us (0.969)
  Pallas kernels: 56.7 us -> 54.9 us
    pallas_call x1, Pallas kernels: 55.8 us -> 54 us  [body(): pl.pallas_call(kernel, out_shape=(jax.ShapeDtypeStruct(flat, f32), jax.Sh...]
where the time goes in v4:
time: 56.8 us; the launch traced here: 56.7 us
  Pallas kernels  54.9 us (97%)
  between operations  1.47 us (3%)
    pallas_call x1, Pallas kernels, body(): pl.pallas_call(kernel, out_shape=(jax.ShapeDtypeStruct(flat, f32), jax.Sh...  54 us

profile of v4, /device:TPU:0, one launch (start us, length us, event | category | flops | bytes accessed | tf_op | source)
XLA Modules:
  0.0 56.7 jit_solution(13821335137137873041)
XLA Ops:
  0.6 0.0 copy-start.10
  0.6 0.0 copy-start.18
  0.7 0.0 copy-start.19
  0.7 0.0 copy-start.1
  0.7 0.0 copy-start
  0.7 0.0 copy-start.3
  0.7 54.0 %shard_map.81 = (f32[768,128]{1,0:T(8,128)S(1)}, f32[768,128]{1,0:T(8,128)S(1)}, s32[1]{0:T(128)}) custom-call(f32[3,16,2048]{2,1,0:T(8,128)} %beam.1, s32[8,32,128]{2,1,0:T(8,128)} %loc_in.1, f32[8,32,128]{2,1,0:T(8,128)} %share_in.1, f32[768,128]{1,0:T(8,128)} %bitcast.38, f32[768,128]{1,0:T(8,128)} %bitcast.37, f32[768,128]{1,0:T(8,128)} %bitcast.39), custom_call_target="tpu_custom_call" | custom-call | tf_op jit(solution)/shard_map/pallas_call | solution.py:876
  55.3 0.0 copy-done.10
  55.3 0.0 copy-done.18
  55.3 0.0 copy-done.19
  55.3 0.0 copy-done.1
  55.3 0.0 copy-done
  55.4 0.0 copy-done.3
  55.4 1.1 %conditional.1 = (f32[24,32,128]{2,1,0:T(8,128)}, f32[24,32,128]{2,1,0:T(8,128)}) conditional(s32[]{:T(128)} %bitcast.24, (f32[768,128]{1,0:T(8,128)S(1)}, f32[768,128]{1,0:T(8,128)S(1)}) %tuple.27, (f32[24,32,128]{2,1,0:T(8,128)S(1)}, f32[24,32,128]{2,1,0:T(8,128)S(1)}, f32[3,16,2048]{2,1,0:T(8,128)S(1)}, s32[8,32,128]{2,1,0:T(8,128)S(1)}, ...), branch_computations={%region_0.0_spmd, %region_1.29_spmd} | conditional | flops 49728704 | bytes 95354696 | solution.py:898
  55.4 0.9 %branch_0_fun.1 = (f32[768,128]{1,0:T(8,128)}, f32[768,128]{1,0:T(8,128)}) custom-call(f32[768,128]{1,0:T(8,128)S(1)} %get-tuple-element.52.a_in, f32[768,128]{1,0:T(8,128)S(1)} %get-tuple-element.53.b_in), custom_call_target="tpu_custom_call" | custom-call | tf_op jit(solution)/shard_map/cond/branch_0_fun/pallas_call | solution.py:808
Async XLA Ops:
  0.6 54.7 %copy-start.10 = (f32[3,16,2048]{2,1,0:T(8,128)S(1)}, f32[3,16,2048]{2,1,0:T(8,128)}, u32[]{:S(2)}) copy-start(f32[3,16,2048]{2,1,0:T(8,128)} %beam.1) | copy-start | bytes 1179652
  0.6 54.7 %copy-start.18 = (s32[8,32,128]{2,1,0:T(8,128)S(1)}, s32[8,32,128]{2,1,0:T(8,128)}, u32[]{:S(2)}) copy-start(s32[8,32,128]{2,1,0:T(8,128)} %loc_in.1) | copy-start | bytes 393220
  0.7 54.7 %copy-start.19 = (f32[8,32,128]{2,1,0:T(8,128)S(1)}, f32[8,32,128]{2,1,0:T(8,128)}, u32[]{:S(2)}) copy-start(f32[8,32,128]{2,1,0:T(8,128)} %share_in.1) | copy-start | bytes 393220
  0.7 54.7 %copy-start.1 = (f32[24,32,128]{2,1,0:T(8,128)S(1)}, f32[24,32,128]{2,1,0:T(8,128)}, u32[]{:S(2)}) copy-start(f32[24,32,128]{2,1,0:T(8,128)} %param.17) | copy-start | bytes 1179652
  0.7 54.7 %copy-start = (f32[24,32,128]{2,1,0:T(8,128)S(1)}, f32[24,32,128]{2,1,0:T(8,128)}, u32[]{:S(2)}) copy-start(f32[24,32,128]{2,1,0:T(8,128)} %param.18) | copy-start | bytes 1179652
  0.7 54.7 %copy-start.3 = (f32[24,32,128]{2,1,0:T(8,128)S(1)}, f32[24,32,128]{2,1,0:T(8,128)}, u32[]{:S(2)}) copy-start(f32[24,32,128]{2,1,0:T(8,128)} %param.19) | copy-start | bytes 1179652

commit v5 on v4

--- a/solution.py
+++ b/solution.py
@@ -188,7 +188,7 @@
 
 
 GHOSTS = (0, 1, NX + 2, NX + 3)
-EXCHANGES = ((1, NZ), (1, NZ), (2, 8))
+EXCHANGES = ((1, 8), (2, 8))
 CORNERS = ((-1, 1), (-1, -1), (1, 1), (1, -1))
 
 
@@ -399,19 +399,24 @@
     exchanges = [
         Exchange(place, exchange_refs[6 * n : 6 * n + 6]) for n in range(len(EXCHANGES))
     ]
-    z_swap, e_swap, f_swap = exchanges
+    tile_swap, f_swap = exchanges
+    ze_swap = PairExchange(place, exchange_refs[-20:-14])
+    ze_edge = exchange_refs[-14]
     first = FirstExchange(place, exchange_refs[-13:-7])
     k_edge = exchange_refs[-7]
     uv_refs = exchange_refs[-6:]
     k_edges = k_edge.at[0], k_edge.at[1]
-    z_edges = z_ref.at[pl.ds(2, 2)], z_ref.at[pl.ds(NX, 2)]
-    e_edges = e_ref.at[pl.ds(2, 2)], e_ref.at[pl.ds(NX, 2)]
+    tile_edges = fd_ref.at[0, pl.ds(2, 2)], fd_ref.at[0, pl.ds(NX, 2)]
+    ze_edges = ze_edge.at[0], ze_edge.at[1]
     f_edges = fd_ref.at[pl.ds(1, 2), pl.ds(2, 2)], fd_ref.at[pl.ds(1, 2), pl.ds(NX, 2)]
     uv_edges = uv_ref.at[:, pl.ds(2, 2)], uv_ref.at[:, pl.ds(NX, 2)]
 
     for copy in local[:3]:
         copy.wait()
     zero = jnp.zeros((NZ, NY), jnp.float32)
+
+    def folded(v):
+        return v[0:8] + v[8:16] + v[16:24]
 
     def zero_row():
         return jnp.zeros((8, NY), jnp.float32)
@@ -545,7 +550,7 @@
         e_ref[x + 2] = e
         return packed_into(pack, e, x)
 
-    e_swap.pack[0] = slabs_loop(conduct_inside, zero)
+    e_pack = slabs_loop(conduct_inside, zero)
 
     below, above, inner, outer = around_halo(k_halo, k_corner, k_pack)
     j = lax.rem(lanes(), 4)
@@ -575,7 +580,14 @@
         x_ref[x] = t
         return packed_into(carry, z, x)
 
-    z_near[2] = slabs_loop(residual, zero)
+    z_pack = slabs_loop(residual, zero)
+    z_near[2] = z_pack
+    ze_swap.fill(z_pack, e_pack)
+    for n in range(2):
+        for m, ref in enumerate((z_ref, e_ref)):
+            ze_edge[0, m, n] = ref[2 + n]
+            ze_edge[1, m, n] = ref[NX + n]
+    ze_swap.start(*ze_edges)
     first.sent(*k_edges)
 
     own_beam.wait()
@@ -627,9 +639,6 @@
             for n in range(len(moments))
         ]
 
-    def folded(v):
-        return v[0:8] + v[8:16] + v[16:24]
-
     frame_bytes(0, beam_recv).wait()
 
     def add_flux(x, pack):
@@ -638,14 +647,59 @@
         z_ref[x + 2, NZ - 8 : NZ, :] = z_ref[x + 2, NZ - 8 : NZ, :] + tile
         return packed_into(pack, tile, x)
 
-    z_near[2, NZ - 8 : NZ] = z_near[2, NZ - 8 : NZ] + slabs_loop(add_flux, zero_row())
-    z_swap.pack[0] = z_near[2]
-    z_swap.start(*z_edges)
-    e_swap.start(*e_edges)
-    z_swap.arrive(*z_edges)
-    for at, slab in zip(GHOSTS, z_swap.slabs(0)):
-        z_ref[at] = slab
-    z_near[0], z_near[1] = z_swap.halo(0), z_swap.corner(0)
+    top = pl.ds(NZ - 8, 8)
+    tile_pack = slabs_loop(add_flux, zero_row())
+    tile_swap.pack[0] = tile_pack
+    tile_swap.start(*tile_edges)
+    z_near[2, top] = z_near[2, top] + tile_pack
+    ze_swap.arrive(*ze_edges)
+    for at, z, e in zip(GHOSTS, ze_swap.slabs(0), ze_swap.slabs(1)):
+        z_ref[at] = z
+        e_ref[at] = e
+    for near, n in ((z_near, 0), (e_near, 1)):
+        near[0], near[1] = ze_swap.halo(n), ze_swap.corner(n)
+
+    dry_halo = z_near[0]
+
+    def early_image(x, carry):
+        sums, pack = carry
+        u = apply_slab(z_ref, x + 2, side_tile(dry_halo, x), g_ref, x + 1)
+        u_ref[x + 2] = u
+        z = z_ref[x + 2]
+        dz = d_ref[x] * z
+        zu, uu = dz * u, d_ref[x] * u * u
+        sums = (
+            sums[0] + folded(dz * z),
+            sums[1] + (zu[0:8] + zu[8:16]),
+            sums[2] + (uu[0:8] + uu[8:16]),
+        )
+        return sums, packed_into(pack, u, x)
+
+    early_sums, early_pack = slabs_loop(early_image, ((zero_row(),) * 3, zero))
+    tile_swap.arrive(*tile_edges)
+    tiles = tile_swap.slabs(0)
+    for at, tile in zip(GHOSTS, tiles):
+        z_ref[at, top] = z_ref[at, top] + tile
+    tile_halo = tile_swap.halo(0)
+    for n, tile in enumerate((tile_halo, tile_swap.corner(0))):
+        z_near[n, top] = z_near[n, top] + tile
+    u_ref[2, top] = u_ref[2, top] - g_ref[2, 1, top] * tiles[1]
+    u_ref[NX + 1, top] = u_ref[NX + 1, top] - g_ref[3, NX, top] * tiles[2]
+
+    def late_image(x, carry):
+        sums, pack = carry
+        side = side_tile(tile_halo, x)
+        near = jnp.where(lane8 == 0, g_ref[4, x + 1, top] * side, 0.0)
+        near = jnp.where(lane8 == NY - 1, g_ref[5, x + 1, top] * side, near)
+        u = u_ref[x + 2, top] - near
+        u_ref[x + 2, top] = u
+        du = d_ref[x, top] * u
+        sums = (sums[0] + du * z_ref[x + 2, top], sums[1] + du * u)
+        return sums, packed_into(pack, u, x)
+
+    late_sums, late_pack = slabs_loop(late_image, (early_sums[1:], zero_row()))
+    early_sums = (early_sums[0], *late_sums)
+    early_pack = jnp.concatenate([early_pack[: NZ - 8], late_pack], axis=0)
 
     def later_fluxes():
         frame_bytes(1, beam_recv).wait()
@@ -683,16 +737,19 @@
                 sums[1] + folded(dz * u),
                 sums[2] + folded(du * u),
             )
-            return sums, packed_into(pack, u, x)
-
-        sums, u_pack = slabs_loop(first_image, ((zero_row(),) * 3, zero))
+            return sums, (packed_into(pack, u, x) if more else pack)
+
+        if step == 0:
+            sums, u_pack = early_sums, early_pack
+        else:
+            sums, u_pack = slabs_loop(first_image, ((zero_row(),) * 3, zero))
 
         def second_image(x, carry):
             acc, pack = carry
             v = apply_slab(u_ref, x + 2, side_tile(u_halo, x), g_ref, x + 1)
             v_ref[x + 2] = v
             acc = acc + folded(d_ref[x] * u_ref[x + 2] * v)
-            return acc, packed_into(pack, v, x)
+            return acc, (packed_into(pack, v, x) if more else pack)
 
         last, v_pack = slabs_loop(second_image, (zero_row(), zero))
 
@@ -709,15 +766,12 @@
         def receive_images():
             @pl.when(step == 0)
             def _():
-                z_swap.sent(*z_edges)
-                e_swap.arrive(*e_edges)
-                for at, slab in zip(GHOSTS, e_swap.slabs(0)):
-                    e_ref[at] = slab
+                ze_swap.sent(*ze_edges)
+                tile_swap.sent(*tile_edges)
                 f_swap.arrive(*f_edges)
                 for n in range(2):
                     for at, slab in zip(GHOSTS, f_swap.slabs(n)):
                         fd_ref[1 + n, at] = slab
-                e_near[0], e_near[1] = e_swap.halo(0), e_swap.corner(0)
                 for n in range(2):
                     f_near[n, 0], f_near[n, 1] = f_swap.halo(n), f_swap.corner(n)
 
@@ -727,10 +781,10 @@
                 for n in range(2):
                     uv_near[n, 0], uv_near[n, 1] = swap.halo(n), swap.corner(n)
 
-        g0, a, w, t, far = all_sum(
-            step, list(sums) + [last, bad], (send_images, receive_images)
-        )
-        flag_out[0] = jnp.where(jnp.sum(far) > 0.0, 1, 0).astype(jnp.int32)
+        moments = list(sums) + [last] + ([bad] if step == 0 else [])
+        g0, a, w, t, *far = all_sum(step, moments, (send_images, receive_images))
+        if step == 0:
+            flag_out[0] = jnp.where(jnp.sum(far[0]) > 0.0, 1, 0).astype(jnp.int32)
         inverse = 1.0 / (a * t - w * w)
         d1 = jnp.broadcast_to((g0 * t - a * w) * inverse, (NZ, NY))
         d2 = jnp.broadcast_to((a * a - g0 * w) * inverse, (NZ, NY))
@@ -770,7 +824,6 @@
 
     for step in range(STEPS):
         one_step(step, 0)
-    e_swap.sent(*e_edges)
     f_swap.sent(*f_edges)
     for frame in range(STEPS):
         frame_bytes(frame, beam_send).wait()
@@ -859,6 +912,13 @@
     for fields, rows in EXCHANGES:
         scratch += exchange_scratch(fields, rows)
     scratch += [
+        pltpu.VMEM((2, 2, 2, NZ, NY), f32),
+        pltpu.VMEM((2, NZ, NY), f32),
+        pltpu.VMEM((4, NZ, NY), f32),
+        pltpu.VMEM((2, NZ, NY), f32),
+        pltpu.SemaphoreType.DMA((8,)),
+        pltpu.SemaphoreType.DMA((8,)),
+        pltpu.VMEM((2, 2, 2, NZ, NY), f32),
         pltpu.VMEM((2, 4, NZ, NY), f32),
         pltpu.VMEM((2, NZ, NY), f32),
         pltpu.VMEM((4, NZ, NY), f32),

time: 56.8 us -> 56.3 us (level)
  no operation moved by 1% of the time
where the time goes in v5:
time: 56.3 us; the launch traced here: 56.2 us
  Pallas kernels  54.5 us (97%)
  between operations  1.47 us (3%)
    pallas_call x1, Pallas kernels, body(): pl.pallas_call(kernel, out_shape=(jax.ShapeDtypeStruct(flat, f32), jax.Sh...  53.6 us

profile of v5, /device:TPU:0, one launch (start us, length us, event | category | flops | bytes accessed | tf_op | source)
XLA Modules:
  0.0 56.2 jit_solution(5233302478160127434)
XLA Ops:
  0.6 0.0 copy-start.10
  0.6 0.0 copy-start.18
  0.7 0.0 copy-start.19
  0.7 0.0 copy-start.1
  0.7 0.0 copy-start
  0.7 0.0 copy-start.3
  0.7 53.6 %shard_map.81 = (f32[768,128]{1,0:T(8,128)S(1)}, f32[768,128]{1,0:T(8,128)S(1)}, s32[1]{0:T(128)}) custom-call(f32[3,16,2048]{2,1,0:T(8,128)} %beam.1, s32[8,32,128]{2,1,0:T(8,128)} %loc_in.1, f32[8,32,128]{2,1,0:T(8,128)} %share_in.1, f32[768,128]{1,0:T(8,128)} %bitcast.38, f32[768,128]{1,0:T(8,128)} %bitcast.37, f32[768,128]{1,0:T(8,128)} %bitcast.39), custom_call_target="tpu_custom_call" | custom-call | tf_op jit(solution)/shard_map/pallas_call | solution.py:936
  54.8 0.0 copy-done.10
  54.8 0.0 copy-done.18
  54.8 0.0 copy-done.19
  54.8 0.0 copy-done.1
  54.9 0.0 copy-done
  54.9 0.0 copy-done.3
  54.9 1.1 %conditional.1 = (f32[24,32,128]{2,1,0:T(8,128)}, f32[24,32,128]{2,1,0:T(8,128)}) conditional(s32[]{:T(128)} %bitcast.24, (f32[768,128]{1,0:T(8,128)S(1)}, f32[768,128]{1,0:T(8,128)S(1)}) %tuple.27, (f32[24,32,128]{2,1,0:T(8,128)S(1)}, f32[24,32,128]{2,1,0:T(8,128)S(1)}, f32[3,16,2048]{2,1,0:T(8,128)S(1)}, s32[8,32,128]{2,1,0:T(8,128)S(1)}, ...), branch_computations={%region_0.0_spmd, %region_1.29_spmd} | conditional | flops 49728704 | bytes 95354696 | solution.py:958
  54.9 0.9 %branch_0_fun.1 = (f32[768,128]{1,0:T(8,128)}, f32[768,128]{1,0:T(8,128)}) custom-call(f32[768,128]{1,0:T(8,128)S(1)} %get-tuple-element.52.a_in, f32[768,128]{1,0:T(8,128)S(1)} %get-tuple-element.53.b_in), custom_call_target="tpu_custom_call" | custom-call | tf_op jit(solution)/shard_map/cond/branch_0_fun/pallas_call | solution.py:861
Async XLA Ops:
  0.6 54.2 %copy-start.10 = (f32[3,16,2048]{2,1,0:T(8,128)S(1)}, f32[3,16,2048]{2,1,0:T(8,128)}, u32[]{:S(2)}) copy-start(f32[3,16,2048]{2,1,0:T(8,128)} %beam.1) | copy-start | bytes 1179652
  0.6 54.2 %copy-start.18 = (s32[8,32,128]{2,1,0:T(8,128)S(1)}, s32[8,32,128]{2,1,0:T(8,128)}, u32[]{:S(2)}) copy-start(s32[8,32,128]{2,1,0:T(8,128)} %loc_in.1) | copy-start | bytes 393220
  0.7 54.2 %copy-start.19 = (f32[8,32,128]{2,1,0:T(8,128)S(1)}, f32[8,32,128]{2,1,0:T(8,128)}, u32[]{:S(2)}) copy-start(f32[8,32,128]{2,1,0:T(8,128)} %share_in.1) | copy-start | bytes 393220
  0.7 54.2 %copy-start.1 = (f32[24,32,128]{2,1,0:T(8,128)S(1)}, f32[24,32,128]{2,1,0:T(8,128)}, u32[]{:S(2)}) copy-start(f32[24,32,128]{2,1,0:T(8,128)} %param.17) | copy-start | bytes 1179652
  0.7 54.2 %copy-start = (f32[24,32,128]{2,1,0:T(8,128)S(1)}, f32[24,32,128]{2,1,0:T(8,128)}, u32[]{:S(2)}) copy-start(f32[24,32,128]{2,1,0:T(8,128)} %param.18) | copy-start | bytes 1179652
  0.7 54.2 %copy-start.3 = (f32[24,32,128]{2,1,0:T(8,128)S(1)}, f32[24,32,128]{2,1,0:T(8,128)}, u32[]{:S(2)}) copy-start(f32[24,32,128]{2,1,0:T(8,128)} %param.19) | copy-start | bytes 1179652

commit v6 on v5

--- a/solution.py
+++ b/solution.py
@@ -648,7 +648,7 @@
         return packed_into(pack, tile, x)
 
     top = pl.ds(NZ - 8, 8)
-    tile_pack = slabs_loop(add_flux, zero_row())
+    tile_pack = slabs_loop(add_flux, zero_row(), 16)
     tile_swap.pack[0] = tile_pack
     tile_swap.start(*tile_edges)
     z_near[2, top] = z_near[2, top] + tile_pack
@@ -697,7 +697,7 @@
         sums = (sums[0] + du * z_ref[x + 2, top], sums[1] + du * u)
         return sums, packed_into(pack, u, x)
 
-    late_sums, late_pack = slabs_loop(late_image, (early_sums[1:], zero_row()))
+    late_sums, late_pack = slabs_loop(late_image, (early_sums[1:], zero_row()), 16)
     early_sums = (early_sums[0], *late_sums)
     early_pack = jnp.concatenate([early_pack[: NZ - 8], late_pack], axis=0)
 
@@ -847,8 +847,9 @@
 
 def hand_on(a_in, b_in, a_out, b_out, sem):
     copies = [
-        pltpu.make_async_copy(src, dst, sem.at[n])
-        for n, (src, dst) in enumerate(((a_in, a_out), (b_in, b_out)))
+        pltpu.make_async_copy(src.at[pl.ds(n * 192, 192)], dst.at[pl.ds(n * 192, 192)], sem.at[m, n])
+        for m, (src, dst) in enumerate(((a_in, a_out), (b_in, b_out)))
+        for n in range(4)
     ]
     for copy in copies:
         copy.start()
@@ -863,7 +864,7 @@
         out_shape=(jax.ShapeDtypeStruct(a.shape, a.dtype), jax.ShapeDtypeStruct(b.shape, b.dtype)),
         in_specs=[space, space],
         out_specs=(space, space),
-        scratch_shapes=[pltpu.SemaphoreType.DMA((2,))],
+        scratch_shapes=[pltpu.SemaphoreType.DMA((2, 4))],
     )(a, b)
 
 

time: 56.3 us -> 56.2 us (level)
  no operation moved by 1% of the time
where the time goes in v6:
time: 56.2 us; the launch traced here: 56 us
  Pallas kernels  54.3 us (97%)
  between operations  1.47 us (3%)
    pallas_call x1, Pallas kernels, body(): pl.pallas_call(kernel, out_shape=(jax.ShapeDtypeStruct(flat, f32), jax.Sh...  53.4 us

profile of v6, /device:TPU:0, one launch (start us, length us, event | category | flops | bytes accessed | tf_op | source)
XLA Modules:
  0.0 56.0 jit_solution(13388794438607656471)
XLA Ops:
  0.6 0.0 copy-start.10
  0.6 0.0 copy-start.18
  0.7 0.0 copy-start.19
  0.7 0.0 copy-start.1
  0.7 0.0 copy-start
  0.7 0.0 copy-start.3
  0.7 53.4 %shard_map.81 = (f32[768,128]{1,0:T(8,128)S(1)}, f32[768,128]{1,0:T(8,128)S(1)}, s32[1]{0:T(128)}) custom-call(f32[3,16,2048]{2,1,0:T(8,128)} %beam.1, s32[8,32,128]{2,1,0:T(8,128)} %loc_in.1, f32[8,32,128]{2,1,0:T(8,128)} %share_in.1, f32[768,128]{1,0:T(8,128)} %bitcast.38, f32[768,128]{1,0:T(8,128)} %bitcast.37, f32[768,128]{1,0:T(8,128)} %bitcast.39), custom_call_target="tpu_custom_call" | custom-call | tf_op jit(solution)/shard_map/pallas_call | solution.py:937
  54.6 0.0 copy-done.10
  54.6 0.0 copy-done.18
  54.6 0.0 copy-done.19
  54.7 0.0 copy-done.1
  54.7 0.0 copy-done
  54.7 0.0 copy-done.3
  54.7 1.2 %conditional.1 = (f32[24,32,128]{2,1,0:T(8,128)}, f32[24,32,128]{2,1,0:T(8,128)}) conditional(s32[]{:T(128)} %bitcast.24, (f32[768,128]{1,0:T(8,128)S(1)}, f32[768,128]{1,0:T(8,128)S(1)}) %tuple.27, (f32[24,32,128]{2,1,0:T(8,128)S(1)}, f32[24,32,128]{2,1,0:T(8,128)S(1)}, f32[3,16,2048]{2,1,0:T(8,128)S(1)}, s32[8,32,128]{2,1,0:T(8,128)S(1)}, ...), branch_computations={%region_0.0_spmd, %region_1.29_spmd} | conditional | flops 49728704 | bytes 95354696 | solution.py:959
  54.7 0.9 %branch_0_fun.1 = (f32[768,128]{1,0:T(8,128)}, f32[768,128]{1,0:T(8,128)}) custom-call(f32[768,128]{1,0:T(8,128)S(1)} %get-tuple-element.52.a_in, f32[768,128]{1,0:T(8,128)S(1)} %get-tuple-element.53.b_in), custom_call_target="tpu_custom_call" | custom-call | tf_op jit(solution)/shard_map/cond/branch_0_fun/pallas_call | solution.py:862
Async XLA Ops:
  0.6 54.0 %copy-start.10 = (f32[3,16,2048]{2,1,0:T(8,128)S(1)}, f32[3,16,2048]{2,1,0:T(8,128)}, u32[]{:S(2)}) copy-start(f32[3,16,2048]{2,1,0:T(8,128)} %beam.1) | copy-start | bytes 1179652
  0.6 54.0 %copy-start.18 = (s32[8,32,128]{2,1,0:T(8,128)S(1)}, s32[8,32,128]{2,1,0:T(8,128)}, u32[]{:S(2)}) copy-start(s32[8,32,128]{2,1,0:T(8,128)} %loc_in.1) | copy-start | bytes 393220
  0.7 54.0 %copy-start.19 = (f32[8,32,128]{2,1,0:T(8,128)S(1)}, f32[8,32,128]{2,1,0:T(8,128)}, u32[]{:S(2)}) copy-start(f32[8,32,128]{2,1,0:T(8,128)} %share_in.1) | copy-start | bytes 393220
  0.7 54.0 %copy-start.1 = (f32[24,32,128]{2,1,0:T(8,128)S(1)}, f32[24,32,128]{2,1,0:T(8,128)}, u32[]{:S(2)}) copy-start(f32[24,32,128]{2,1,0:T(8,128)} %param.17) | copy-start | bytes 1179652
  0.7 54.0 %copy-start = (f32[24,32,128]{2,1,0:T(8,128)S(1)}, f32[24,32,128]{2,1,0:T(8,128)}, u32[]{:S(2)}) copy-start(f32[24,32,128]{2,1,0:T(8,128)} %param.18) | copy-start | bytes 1179652
  0.7 54.0 %copy-start.3 = (f32[24,32,128]{2,1,0:T(8,128)S(1)}, f32[24,32,128]{2,1,0:T(8,128)}, u32[]{:S(2)}) copy-start(f32[24,32,128]{2,1,0:T(8,128)} %param.19) | copy-start | bytes 1179652
